TPU v7x, 256 devices: a whole 4x4x8 slice. The times are simulated.
256 devices in a mesh: section: 4 (over y), tp: 64 (over x, z, core).
Axes of the slice: x: 4, y: 4, z: 8, core: 2. Of those that a mesh axis runs over, the one named last changes fastest.
Arguments:
- tokens: bfloat16 [16, 64, 5120], P('section', None, 'tp'), may hold values from -6 to 6
- language: int32 [16, 1], P('section'), may hold values from 0 to 3; in each aligned block of 4 rows (0 to 3, 4 to 7, ...) at most 2 rows name the same one
- example_ids: int32 [16], P('section'), may hold values from 0 to 15, each once
- history: bfloat16 [16, 64, 5120], P(None, None, 'tp'), may hold values from -6 to 6
- enc_gain: float32 [5120], replicated, may hold values from 0.1 to 1.9
- dec_gain: float32 [4, 5120], P('section'), may hold values from 0.1 to 1.9
- enc_gate: bfloat16 [5120, 20480], P('section', 'tp'), may hold values from -0.078125 to 0.078125
- enc_in: bfloat16 [5120, 20480], P('section', 'tp'), may hold values from -0.078125 to 0.078125
- enc_out: bfloat16 [20480, 5120], P('tp', 'section'), may hold values from -0.0390625 to 0.0390625
- dec_gate: bfloat16 [4, 5120, 20480], P('section', None, 'tp'), may hold values from -0.078125 to 0.078125
- dec_in: bfloat16 [4, 5120, 20480], P('section', None, 'tp'), may hold values from -0.078125 to 0.078125
- dec_out: bfloat16 [4, 20480, 5120], P('section', 'tp'), may hold values from -0.0390625 to 0.0390625
Outputs:
- decoded: bfloat16 [16, 64, 5120], P('section', None, 'tp')
- new_memory: bfloat16 [16, 64, 5120], P('section', None, 'tp')
- quantized: bfloat16 [16, 64, 5120], P('section', None, 'tp')
Inputs may be any that keep to these rules, and one draw needn't show every extreme that they name: In each aligned block of 4 examples (those of one section group) no language is named by more than 2 examples, a bound that some block reaches. `example_ids`: every buffer row is named by exactly one example.
All inputs are finite; a program needn't handle non-finite values. Where the computation divides by a largest or mean magnitude, that divisor is 1e-20 or more.
Results may differ from a plain program's by a relative error of at most 0.015.
Values may be sent and summed in bfloat16 or wider, within the bound.
A program may use at most 128 MiB of HBM per device.

v0:
```python
import jax
import jax.numpy as jnp
from jax import lax
from jax.sharding import PartitionSpec as P

epsilon = 1e-06


def rms_norm(values, gain):
    wide = values.astype(jnp.float32)
    return wide * lax.rsqrt(jnp.mean(wide * wide, axis=-1, keepdims=True) + epsilon) * gain


def shards(
    tokens,
    language,
    example_ids,
    history,
    enc_gain,
    dec_gain,
    enc_gate,
    enc_in,
    enc_out,
    dec_gate,
    dec_in,
    dec_out,
):
    ex_local, seq_len, width_part = tokens.shape
    groups = lax.axis_size("section")
    capacity = ex_local // 2
    row_count = ex_local * seq_len
    flattened = tokens.reshape(row_count, width_part)
    gathered = lax.all_gather(flattened, "tp", axis=1, tiled=True)
    normed = rms_norm(gathered, enc_gain).astype(jnp.bfloat16)
    pre_gate = jnp.dot(
        normed,
        lax.all_gather(enc_gate, "section", axis=0, tiled=True),
        preferred_element_type=jnp.float32,
    )
    pre_up = jnp.dot(
        normed,
        lax.all_gather(enc_in, "section", axis=0, tiled=True),
        preferred_element_type=jnp.float32,
    )
    hidden = (jax.nn.gelu(pre_gate) * pre_up).astype(jnp.bfloat16)
    partial_value = jnp.dot(
        hidden,
        lax.all_gather(enc_out, "section", axis=1, tiled=True),
        preferred_element_type=jnp.float32,
    )
    summed = lax.psum_scatter(partial_value, "tp", scatter_dimension=1, tiled=True)
    encoded = (
        (flattened.astype(jnp.float32) + summed)
        .astype(jnp.bfloat16)
        .reshape(ex_local, seq_len, width_part)
    )
    baseline = jnp.take(history, example_ids, axis=0)
    difference = encoded.astype(jnp.float32) - baseline.astype(jnp.float32)
    block_scale = jnp.max(jnp.abs(difference), axis=1, keepdims=True) + epsilon
    quantized = (difference / block_scale).astype(jnp.bfloat16)
    new_memory = (
        baseline.astype(jnp.float32) + quantized.astype(jnp.float32) * block_scale
    ).astype(jnp.bfloat16)
    lang_local = language[:, 0]
    chosen = (lang_local[:, None] == jnp.arange(groups, dtype=jnp.int32)[None, :]).astype(jnp.int32)
    earlier = jnp.cumsum(chosen, axis=0) - chosen
    position = jnp.sum(earlier * chosen, axis=1)
    slot_index = lang_local * capacity + position
    placing = (
        jnp.arange(groups * capacity, dtype=jnp.int32)[:, None] == slot_index[None, :]
    ).astype(jnp.bfloat16)
    packed = jnp.einsum(
        "se,ek->sk",
        placing,
        new_memory.reshape(ex_local, seq_len * width_part),
        preferred_element_type=jnp.float32,
    )
    packed = packed.astype(jnp.bfloat16).reshape(groups, capacity, seq_len * width_part)
    norm_gain = dec_gain[0]
    weight_gate = dec_gate[0]
    weight_in = dec_in[0]
    weight_out = dec_out[0]
    slot_rows = lax.all_to_all(packed, "section", split_axis=0, concat_axis=0, tiled=True)
    row_total = slot_rows.shape[0] * slot_rows.shape[1] * seq_len
    pieces = slot_rows.reshape(row_total, width_part)
    gathered_rows = lax.all_gather(pieces, "tp", axis=1, tiled=True)
    dec_normed = rms_norm(gathered_rows, norm_gain).astype(jnp.bfloat16)
    gate_part = jnp.dot(dec_normed, weight_gate, preferred_element_type=jnp.float32)
    up_part = jnp.dot(dec_normed, weight_in, preferred_element_type=jnp.float32)
    dec_hidden = (jax.nn.gelu(gate_part) * up_part).astype(jnp.bfloat16)
    partial_out = jnp.dot(dec_hidden, weight_out, preferred_element_type=jnp.float32)
    reduced = lax.psum_scatter(partial_out, "tp", scatter_dimension=1, tiled=True)
    output = (pieces.astype(jnp.float32) + reduced).astype(jnp.bfloat16)
    finished = output.reshape(slot_rows.shape)
    returned = lax.all_to_all(finished, "section", split_axis=0, concat_axis=0, tiled=True)
    decoded = jnp.einsum(
        "se,sk->ek",
        placing,
        returned.reshape(groups * capacity, seq_len * width_part),
        preferred_element_type=jnp.float32,
    )
    decoded = decoded.astype(jnp.bfloat16).reshape(ex_local, seq_len, width_part)
    return (decoded, new_memory, quantized)


def solution(mesh):
    in_specs = (
        P("section", None, "tp"),
        P("section", None),
        P("section"),
        P(None, None, "tp"),
        P(),
        P("section", None),
        P("section", "tp"),
        P("section", "tp"),
        P("tp", "section"),
        P("section", None, "tp"),
        P("section", None, "tp"),
        P("section", "tp", None),
    )
    out_specs = (P("section", None, "tp"), P("section", None, "tp"), P("section", None, "tp"))
    return jax.shard_map(shards, mesh=mesh, in_specs=in_specs, out_specs=out_specs, check_vma=False)
```

profile of v0, /device:TPU:2, one launch (start us, length us, event | category | flops | bytes accessed | tf_op | source)
XLA Modules:
  0.0 670.3 jit_solution(12585299844541383935)
XLA Ops:
  7.2 0.0 copy-start
  7.2 0.0 all-gather.6.cloned.1.call-start
  7.2 1.7 copy.29
  8.9 0.0 all-gather.6.cloned.1.call-update
  8.9 0.0 all-gather.8.cloned.1.call-start
  9.0 0.7 all-gather.8.cloned.1.call-update
  9.7 0.0 all-gather.10.cloned.1.call-start
  9.7 0.7 all-gather.10.cloned.1.call-update
  10.4 0.0 all-gather.12.cloned.1.call-start
  10.5 0.5 all-gather.12.cloned.1.call-update
  11.0 0.0 reduce-scatter.3.cloned.1.call-start
  11.1 79.9 %all-gather.6.cloned.1.call-done = bf16[256,5120]{0,1:T(8,128)(2,1)} async-done(((bf16[256,80]{0,1:T(8,128)(2,1)}), bf16[256,5120]{0,1:T(8,128)(2,1)}) %all-gather.6.cloned.1.call-update) | async-done | bytes 2621456 | tf_op jit(solution)/shard_map/all_gather | solution.py:33
  91.0 2.4 fusion.3
  93.4 41.3 %all-gather.8.cloned.1.call-done = bf16[5120,320]{0,1:T(8,128)(2,1)} async-done(((bf16[1280,320]{0,1:T(8,128)(2,1)}), bf16[5120,320]{0,1:T(8,128)(2,1)}) %all-gather.8.cloned.1.call-update) | async-done | bytes 3276816 | tf_op jit(solution)/shard_map/all_gather | solution.py:37
  134.8 4.7 fusion.47
  139.5 40.5 %all-gather.10.cloned.1.call-done = bf16[5120,320]{0,1:T(8,128)(2,1)} async-done(((bf16[1280,320]{0,1:T(8,128)(2,1)}), bf16[5120,320]{0,1:T(8,128)(2,1)}) %all-gather.10.cloned.1.call-update) | async-done | bytes 3276816 | tf_op jit(solution)/shard_map/all_gather | solution.py:42
  180.0 45.1 %all-gather.12.cloned.1.call-done = bf16[320,5120]{1,0:T(8,128)(2,1)} async-done(((bf16[320,1280]{1,0:T(8,128)(2,1)}), bf16[320,5120]{1,0:T(8,128)(2,1)}) %all-gather.12.cloned.1.call-update) | async-done | bytes 3276816 | tf_op jit(solution)/shard_map/all_gather | solution.py:48
  225.2 0.0 copy-done.4
  225.2 10.3 %fusion.25 = f32[256,5120]{0,1:T(8,128)} fusion(bf16[320,5120]{1,0:T(8,128)(2,1)} %all-gather.12.cloned.1.call-done, f32[256,320]{0,1:T(8,128)} %fusion.47, bf16[5120,320]{0,1:T(8,128)(2,1)} %all-gather.10.cloned.1.call-done, bf16[256,5120]{0,1:T(8,128)(2,1)} %all-gather.6.cloned.1.call-done, f32[5120]{0:T(1024)S(1)} %copy-done.4, f32[256]{0:T(256)S(1)} %add_rsqrt_fusion.1), kind=kOutput, calls=%fused_computation.23 | convolution fusion | flops 1683128320 | bytes 14767104 | tf_op jit(solution)/shard_map/dot_general | solution.py:46
  235.5 0.0 reduce-scatter.3.cloned.1.call-update
  235.5 0.0 all-gather.14.cloned.1.call-start
  235.5 0.6 copy-done.9
  236.1 1.5 gather_fusion
  237.6 0.8 gather.7
  238.4 0.0 copy-done.6
  238.4 0.1 fusion.59
  238.5 0.2 select_reduce_fusion
  238.7 0.5 compare_and_fusion
  239.3 0.5 multiply_add_fusion
  239.7 140.6 %reduce-scatter.3.cloned.1.call-done = f32[256,80]{0,1:T(8,128)} async-done(((f32[256,5120]{0,1:T(8,128)}), f32[256,80]{0,1:T(8,128)}) %reduce-scatter.3.cloned.1.call-update) | async-done | bytes 81936 | tf_op jit(solution)/shard_map/reduce_scatter | solution.py:51
  380.4 0.0 copy-done.3
  380.4 0.9 fusion.54
  381.3 0.1 copy.31
  381.4 0.2 reshape.74
  381.5 0.7 abs_reduce_fusion
  382.2 0.0 copy-start.5
  382.3 0.6 copy-done.5
  382.8 0.7 div.27
  383.5 1.7 div.28
  385.2 1.7 convolution_convert_fusion
  386.9 0.9 reshape.69
  387.8 10.0 %all_to_all.10 = bf16[4,2,5120]{2,1,0:T(2,128)(2,1)} all-to-all(bf16[4,2,5120]{2,1,0:T(2,128)(2,1)S(1)} %reshape.69), channel_id=1, replica_groups=mesh['section'=4,'tp'=64] {'section'}, dimensions={0} | all-to-all | bytes 163840 | tf_op jit(solution)/shard_map/all_to_all | solution.py:83
  397.8 1.7 reshape.70
  399.6 1.6 copy.33
  401.2 0.0 all-gather.14.cloned.1.call-update
  401.2 0.2 reduce-scatter.5.cloned.1.call-start
  401.4 75.9 %all-gather.14.cloned.1.call-done = bf16[512,5120]{0,1:T(8,128)(2,1)} async-done(((bf16[512,80]{0,1:T(8,128)(2,1)}), bf16[512,5120]{0,1:T(8,128)(2,1)}) %all-gather.14.cloned.1.call-update) | async-done | bytes 5242896 | tf_op jit(solution)/shard_map/all_gather | solution.py:86
  477.4 3.8 fusion
  481.1 0.0 copy-done.8
  481.2 0.2 copy-done.1
  481.4 4.3 fusion.36
  485.7 2.1 fusion.19
  487.7 0.0 copy-done
  487.7 5.6 fusion.6
  493.3 0.0 reduce-scatter.5.cloned.1.call-update
  493.4 153.5 %reduce-scatter.5.cloned.1.call-done = f32[512,80]{0,1:T(8,128)} async-done(((f32[512,5120]{0,1:T(8,128)}), f32[512,80]{0,1:T(8,128)}) %reduce-scatter.5.cloned.1.call-update) | async-done | bytes 163856 | tf_op jit(solution)/shard_map/reduce_scatter | solution.py:92
  646.9 1.6 add_convert_fusion
  648.5 1.6 copy.35
  650.1 1.8 reshape.71
  651.9 4.3 all-to-all-start.1
  656.2 1.4 fusion.50
  657.6 4.3 all-to-all-done.1
  661.9 0.8 convolution_convert_fusion.1
  662.7 0.8 reshape.73
  (17 shorter events, 0.1 us)
Async XLA Ops:
  7.2 480.6 %copy-start = (bf16[1,320,5120]{2,1,0:T(8,128)(2,1)S(1)}, bf16[1,320,5120]{2,1,0:T(8,128)(2,1)}, u32[]{:S(2)}) copy-start(bf16[1,320,5120]{2,1,0:T(8,128)(2,1)} %param.23) | copy-start | bytes 9830404
  7.2 83.8 %all-gather.6.cloned.1.call-start = ((), (), s32[]{:S(2)}) async-start(), calls=%async_computation.4 | async-start | bytes 2662400 | tf_op jit(solution)/shard_map/all_gather | solution.py:33
  8.9 125.8 %all-gather.8.cloned.1.call-start = ((), (), s32[]{:S(2)}) async-start(), calls=%async_computation.5 | async-start | bytes 4096000 | tf_op jit(solution)/shard_map/all_gather | solution.py:37
  9.7 170.3 %all-gather.10.cloned.1.call-start = ((), (), s32[]{:S(2)}) async-start(), calls=%async_computation.6 | async-start | bytes 4096000 | tf_op jit(solution)/shard_map/all_gather | solution.py:42
  10.4 214.7 %all-gather.12.cloned.1.call-start = ((), (), s32[]{:S(2)}) async-start(), calls=%async_computation.7 | async-start | bytes 4096000 | tf_op jit(solution)/shard_map/all_gather | solution.py:48
  11.0 369.3 %reduce-scatter.3.cloned.1.call-start = ((), (), s32[]{:S(2)}) async-start(), calls=%async_computation.8 | async-start | bytes 5324800 | tf_op jit(solution)/shard_map/reduce_scatter | solution.py:51
  93.4 131.7 %copy-start.4 = (f32[5120]{0:T(1024)S(1)}, f32[5120]{0:T(1024)}, u32[]{:S(2)}) copy-start(f32[5120]{0:T(1024)} %param.16) | copy-start | bytes 61444
  235.5 0.7 copy-start.9
  235.5 3.0 copy-start.6
  235.5 144.9 %copy-start.3 = (bf16[256,80]{0,1:T(8,128)(2,1)S(1)}, bf16[256,80]{0,1:T(8,128)(2,1)}, u32[]{:S(2)}) copy-start(bf16[256,80]{0,1:T(8,128)(2,1)} %copy.29) | copy-start | bytes 122884
  235.5 241.9 %all-gather.14.cloned.1.call-start = ((), (), s32[]{:S(2)}) async-start(), calls=%async_computation.9 | async-start | bytes 5324800 | tf_op jit(solution)/shard_map/all_gather | solution.py:86
  382.2 0.6 copy-start.5
  397.8 83.3 %copy-start.8 = (f32[1,5120]{1,0:T(1,128)S(1)}, f32[1,5120]{1,0:T(1,128)}, u32[]{:S(2)}) copy-start(f32[1,5120]{1,0:T(1,128)} %param.17) | copy-start | bytes 61444
  401.2 245.7 %reduce-scatter.5.cloned.1.call-start = ((), (), s32[]{:S(2)}) async-start(), calls=%async_computation.10 | async-start | bytes 10649600 | tf_op jit(solution)/shard_map/reduce_scatter | solution.py:92
  477.4 4.0 copy-start.1
  481.4 4.3 copy-start.7
  493.3 153.6 %copy-start.2 = (bf16[512,80]{0,1:T(8,128)(2,1)S(1)}, bf16[512,80]{0,1:T(8,128)(2,1)}, u32[]{:S(2)}) copy-start(bf16[512,80]{0,1:T(8,128)(2,1)} %copy.33) | copy-start | bytes 245764
  651.9 10.0 %all-to-all-start.1 = ((bf16[4,2,5120]{2,1,0:T(2,128)(2,1)}), bf16[4,2,5120]{2,1,0:T(2,128)(2,1)S(1)}, u32[]{:S(2)}, u32[]{:S(2)}) async-start(bf16[4,2,5120]{2,1,0:T(2,128)(2,1)} %reshape.71), calls=%async_computation.3 | async-start | bytes 163840 | tf_op jit(solution)/shard_map/all_to_all | solution.py:95
Sparse Core Ops, SparseCore 0:
  11.3 79.5 all-gather.5
  92.8 41.9 all-gather.7
  136.6 43.4 all-gather.9
  181.7 43.4 all-gather.11
  235.6 144.6 reduce-scatter.2
  401.3 75.9 all-gather.13
  493.5 153.3 reduce-scatter.4
where the time goes:
time: 671 us; the launch traced here: 670 us
  waiting for transfers between devices  583 us (87%)
  matrix products  29.5 us (4%)
  local copies, waits for them, and re-layouts  16.5 us (2%)
  between operations  14.2 us (2%)
  other arithmetic  12.2 us (2%)
  blocking collectives  9.99 us (1%)
    reduce_scatter x1, waiting for transfers between devices, shards(): lax.psum_scatter(partial_out, 'tp', scatter_dimension=1, tiled=True)  154 us
    reduce_scatter x1, waiting for transfers between devices, shards(): lax.psum_scatter(partial_value, 'tp', scatter_dimension=1, tiled=True)  141 us
    all_gather x1, waiting for transfers between devices, shards(): gathered = lax.all_gather(flattened, 'tp', axis=1, tiled=True)  79.9 us
    all_gather x1, waiting for transfers between devices, shards(): gathered_rows = lax.all_gather(pieces, 'tp', axis=1, tiled=True)  75.9 us
    all_gather x1, waiting for transfers between devices, shards(): lax.all_gather(enc_out, 'section', axis=1, tiled=True)  45.1 us
    all_gather x1, waiting for transfers between devices, shards(): lax.all_gather(enc_gate, 'section', axis=0, tiled=True)  41.3 us
    all_gather x1, waiting for transfers between devices, shards(): lax.all_gather(enc_in, 'section', axis=0, tiled=True)  40.5 us
  transfers between devices with their start and end apart: 8, of which 8 were waited for; matrix products, arithmetic and copies ran while one was open for 2% of the time, Pallas kernels for 0%

commit v1 on v0

v1 whole, which is shorter than its diff:
```python
import functools

import jax
import jax.numpy as jnp
from jax import lax
from jax.experimental import pallas as pl
from jax.experimental.pallas import tpu as pltpu
from jax.sharding import PartitionSpec as P

MESH = pl.DeviceIdType.MESH
BF16 = jnp.bfloat16
F32 = jnp.float32
EPS = 1e-06
NX, NZ, NY = 4, 8, 4
SEQ = 64
PART = 80
HEAD = 48
TAIL = PART - HEAD
SLICE = 1280
UNITS = 320
WIDTH = 5120
COPIES = 112


class Links:
    def __init__(self, send_sem, recv_sem):
        self.send_sem, self.recv_sem = send_sem, recv_sem
        self.count = 0
        self.sent = []

    def start(self, src, dst, device):
        copy = pltpu.make_async_remote_copy(
            src_ref=src,
            dst_ref=dst,
            send_sem=self.send_sem.at[self.count],
            recv_sem=self.recv_sem.at[self.count],
            device_id=device,
            device_id_type=MESH,
        )
        self.count += 1
        copy.start()
        self.sent.append(copy)
        return copy

    def finish(self):
        for copy in self.sent:
            copy.wait_send()
        self.sent = []


class Place:
    def __init__(self):
        self.y = lax.axis_index("section")
        t = lax.axis_index("tp")
        self.x, self.z, self.c = t // 16, (t // 2) % 8, t % 2
        self.d = 1 - 2 * self.c

    def at(self, y=None, x=None, z=None, c=None):
        y = self.y if y is None else y
        x = self.x if x is None else x
        z = self.z if z is None else z
        c = self.c if c is None else c
        return (y, (x * 8 + z) * 2 + c)

    def xo(self, off):
        return (self.x + off + 8) % 4

    def yo(self, off):
        return (self.y + off + 8) % 4

    def zo(self, off):
        return (self.z + self.d * off + 16) % 8

    def plane(self):
        return [
            self.at(z=self.zo(1)),
            self.at(z=self.zo(-1)),
            self.at(x=self.xo(1)),
            self.at(x=self.xo(-1)),
            self.at(c=1 - self.c),
        ]

    def column(self):
        return [self.at(y=self.yo(k)) for k in (1, 2, 3)]


ORDER = (0, -1, 1, -2, 2, -3, 3, -4)
TARGETS = (4, -3, 3, -2, 2, -1, 1, 0)


def gather_plane(links, me, blocks):
    zp, zm, xp, xm, partner = me.plane()
    x, z, c = me.x, me.z, me.c

    def head(xx, off):
        return blocks.at[xx, me.zo(off), c, pl.ds(0, HEAD)]

    def tail(xx):
        return blocks.at[xx, z, c, pl.ds(HEAD, TAIL)]

    def heads(off):
        return blocks.at[:, me.zo(off), c, pl.ds(0, HEAD)]

    def tails(off):
        return blocks.at[:, me.zo(off), c, pl.ds(HEAD, TAIL)]

    along, tail_along, cross, second, core = {}, {}, {}, {}, []

    def head_z(off):
        if -4 < off <= 0:
            along[off - 1] = links.start(head(x, off), head(x, off), zp)
        if 0 <= off < 3:
            along[off + 1] = links.start(head(x, off), head(x, off), zm)

    def head_x(off):
        cross[off] = (
            links.start(head(x, off), head(x, off), xp),
            links.start(head(x, off), head(x, off), xm),
        )

    def tail_z(off):
        if -4 < off <= 0:
            tail_along[off - 1] = links.start(tails(off), tails(off), zp)
        if 0 <= off < 3:
            tail_along[off + 1] = links.start(tails(off), tails(off), zm)

    def to_core(ref):
        core.append(links.start(ref, ref, partner))

    def hop(index):
        off = ORDER[index]
        cross[off][0].wait_recv()
        cross[off][1].wait_recv()
        if index % 2 == 0:
            second[off] = links.start(head(me.xo(-1), off), head(me.xo(-1), off), xp)
        else:
            second[off] = links.start(head(me.xo(1), off), head(me.xo(1), off), xm)

    def land(index):
        off = ORDER[index]
        second[off].wait_recv()
        to_core(heads(off))

    def tail_step(index):
        off = ORDER[index]
        tail_along[off].wait_recv()
        tail_z(off)
        to_core(tails(off))

    head_z(0)
    tail_x = (links.start(tail(x), tail(x), xp), links.start(tail(x), tail(x), xm))
    head_x(0)
    for i in range(1, 8):
        off = ORDER[i]
        along[off].wait_recv()
        head_z(off)
        head_x(off)
        if i == 1:
            tail_x[0].wait_recv()
            tail_x[1].wait_recv()
            onward = tail(me.xo(-me.d))
            tail_second = links.start(onward, onward, me.at(x=me.xo(me.d)))
        if i == 2:
            tail_second.wait_recv()
            tail_z(0)
            to_core(tails(0))
        if i >= 4:
            tail_step(i - 3)
        hop(i - 1)
        if i >= 2:
            land(i - 2)
    hop(7)
    tail_step(5)
    land(6)
    tail_step(6)
    land(7)
    tail_step(7)
    for copy in core:
        copy.wait_recv()


def add_to(dst, *terms):
    total = dst[...].astype(F32)
    for term in terms:
        total = total + term[...].astype(F32)
    dst[...] = total.astype(dst.dtype)


def scatter_shapes(rows):
    return [
        pltpu.VMEM((NX, NZ, 2, PART, rows), BF16),
        pltpu.VMEM((NX, NZ, PART, rows), BF16),
        pltpu.VMEM((8, HEAD, rows), BF16),
        pltpu.VMEM((8, 2, HEAD, rows), BF16),
        pltpu.VMEM((4, HEAD, rows), BF16),
        pltpu.VMEM((3, HEAD, rows), BF16),
        pltpu.VMEM((4, NX, TAIL, rows), BF16),
        pltpu.VMEM((3, NX, TAIL, rows), BF16),
        pltpu.VMEM((TAIL, rows), BF16),
        pltpu.VMEM((2, TAIL, rows), BF16),
        pltpu.VMEM((PART, rows), F32),
    ]


def scatter_plane(links, me, bufs, core_copies):
    sums, theirs, first, both, up_z, down_z, up_tail, down_tail, tail_first, tail_both, result = bufs
    zp, zm, xp, xm, _ = me.plane()
    x, z, c, d = me.x, me.z, me.c, me.d

    def head(xx, off):
        return sums.at[xx, me.zo(off), c, pl.ds(0, HEAD)]

    def tail(xx):
        return sums.at[xx, z, c, pl.ds(HEAD, TAIL)]

    def tails(off):
        return sums.at[:, me.zo(off), c, pl.ds(HEAD, TAIL)]

    for xx, copy in core_copies:
        copy.wait_recv()
        add_to(sums.at[xx, :, c], theirs.at[xx])

    hops, direct, relayed, along, tail_along = {}, {}, {}, {}, {}
    for i, off in enumerate(TARGETS):
        e = 1 if i % 2 == 0 else -1
        ahead, behind = (xp, xm) if e == 1 else (xm, xp)
        hops[i] = links.start(head(me.xo(2), off), first.at[i], ahead)
        direct[i] = links.start(head(me.xo(-e), off), both.at[i, 1], behind)
        if i == 0:
            tail_along[4] = links.start(tails(4), up_tail.at[0], zp)
            tail_along[-3] = links.start(tails(-3), down_tail.at[0], zm)

    def relay(i):
        off = TARGETS[i]
        e = 1 if i % 2 == 0 else -1
        hops[i].wait_recv()
        add_to(head(me.xo(e), off), first.at[i])
        relayed[i] = links.start(head(me.xo(e), off), both.at[i, 0], xp if e == 1 else xm)

    def tail_step(off):
        if off > 0:
            tail_along[off + 1].wait_recv()
            add_to(tails(off), up_tail.at[3 - off])
            tail_along[off] = links.start(tails(off), up_tail.at[4 - off], zp)
        else:
            tail_along[off - 1].wait_recv()
            add_to(tails(off), down_tail.at[2 + off])
            tail_along[off] = links.start(tails(off), down_tail.at[3 + off], zm)

    def collect(i):
        off = TARGETS[i]
        relayed[i].wait_recv()
        direct[i].wait_recv()
        if off == 4:
            add_to(head(x, off), both.at[i, 0], both.at[i, 1])
            along[4] = links.start(head(x, off), up_z.at[0], zp)
        elif off == -3:
            add_to(head(x, off), both.at[i, 0], both.at[i, 1])
            along[-3] = links.start(head(x, off), down_z.at[0], zm)
        elif off > 0:
            along[off + 1].wait_recv()
            add_to(head(x, off), both.at[i, 0], both.at[i, 1], up_z.at[3 - off])
            along[off] = links.start(head(x, off), up_z.at[4 - off], zp)
        elif off < 0:
            along[off - 1].wait_recv()
            add_to(head(x, off), both.at[i, 0], both.at[i, 1], down_z.at[2 + off])
            along[off] = links.start(head(x, off), down_z.at[3 + off], zm)

    relay(0)
    relay(1)
    for i in range(2, 8):
        relay(i)
        if i < 7:
            tail_step(TARGETS[i])
        collect(i - 2)
    tail_along[1].wait_recv()
    tail_along[-1].wait_recv()
    add_to(tails(0), up_tail.at[3], down_tail.at[2])
    tail_hop = links.start(tail(me.xo(2)), tail_first, me.at(x=me.xo(d)))
    tail_direct = links.start(tail(me.xo(-d)), tail_both.at[1], me.at(x=me.xo(-d)))
    collect(6)
    tail_hop.wait_recv()
    add_to(tail(me.xo(d)), tail_first)
    tail_relayed = links.start(tail(me.xo(d)), tail_both.at[0], me.at(x=me.xo(d)))
    relayed[7].wait_recv()
    direct[7].wait_recv()
    along[1].wait_recv()
    along[-1].wait_recv()
    result[pl.ds(0, HEAD)] = (
        head(x, 0)[...].astype(F32)
        + both[7, 0].astype(F32)
        + both[7, 1].astype(F32)
        + up_z[3].astype(F32)
        + down_z[2].astype(F32)
    )
    tail_relayed.wait_recv()
    tail_direct.wait_recv()
    result[pl.ds(HEAD, TAIL)] = (
        tail(x)[...].astype(F32) + tail_both[0].astype(F32) + tail_both[1].astype(F32)
    )


def contract(a, b):
    return lax.dot_general(a, b, (((0,), (0,)), ((), ())), preferred_element_type=F32)


def gelu(v):
    return jax.nn.gelu(v)


def scale_rows(weights, gain_ref, first_row, count):
    def step(i, carry):
        rows = pl.ds(pl.multiple_of(i * 128, 128), 128)
        line = gain_ref[pl.ds(first_row + i, 1), :]
        column = jnp.broadcast_to(line, (128, 128)).T[:, 0:1]
        for ref in weights:
            ref[rows, :] = (ref[rows, :].astype(F32) * column).astype(BF16)
        return carry

    lax.fori_loop(0, count, step, 0)


def greet(me, senders, receivers_count, extra=None):
    barrier = pltpu.get_barrier_semaphore()
    for device in senders:
        pl.semaphore_signal(barrier, inc=1, device_id=device, device_id_type=MESH)
    if extra is not None:
        extra(barrier)
    pl.semaphore_wait(barrier, receivers_count)


def encoder_kernel(
    tokens_ref, history_ref, ids_ref, language_ref, gain_ref, gate_hbm, in_hbm, out_hbm,
    all_ref, memory_ref, quantized_ref, languages_ref,
    turned, base, blocks, w_gate, w_in, w_out, pre_send, relay_in, pre_in, pre_own,
    squares, squares_in, hidden, lang_send, code_pair, code_in, memory_all, lang_all,
    sums, theirs, first, both, up_z, down_z, up_tail, down_tail, tail_first, tail_both, result,
    send_sem, recv_sem, turn_sem, fan_send, fan_recv, load_sem,
):
    me = Place()
    x, y, z, c = me.x, me.y, me.z, me.c
    links = Links(send_sem, recv_sem)
    diagonal = x == y

    loads = [
        pltpu.make_async_copy(src, dst, load_sem.at[i])
        for i, (src, dst) in enumerate(((gate_hbm, w_gate), (in_hbm, w_in), (out_hbm, w_out)))
    ]
    for load in loads:
        load.start()

    def fan(barrier):
        for g in range(4):
            @pl.when(jnp.logical_not(jnp.logical_and(diagonal, x == g)))
            def _():
                pl.semaphore_signal(barrier, inc=1, device_id=me.at(y=x, x=g), device_id_type=MESH)

    turned[0] = tokens_ref[...].reshape(256, PART).T
    for e in range(4):
        turned[1, :, pl.ds(e * SEQ, SEQ)] = history_ref[ids_ref[e]].T
    lane = lax.broadcasted_iota(jnp.int32, (8, 128), 1)
    lines = jnp.zeros((8, 128), jnp.int32)
    for e in range(4):
        lines = jnp.where(lane == e, language_ref[e, 0], lines)
    lang_send[...] = lines

    greet(me, me.plane() + me.column(), jnp.where(diagonal, 11, 12), fan)

    other = me.at(y=x, x=y)
    turns = [
        pltpu.make_async_remote_copy(
            src_ref=turned.at[i], dst_ref=dst, send_sem=turn_sem.at[0, i], recv_sem=turn_sem.at[1, i],
            device_id=other, device_id_type=MESH)
        for i, dst in enumerate((blocks.at[y, z, c], base))
    ]

    @pl.when(jnp.logical_not(diagonal))
    def _():
        for turn in turns:
            turn.start()

    @pl.when(diagonal)
    def _():
        blocks[x, z, c] = turned[0]
        base[...] = turned[1]

    lang_copies = [links.start(lang_send, lang_all.at[y], me.at(y=me.yo(k))) for k in (1, 2, 3)]

    @pl.when(jnp.logical_not(diagonal))
    def _():
        turns[0].wait_recv()

    loads[0].wait()
    loads[1].wait()
    scale_rows((w_gate, w_in), gain_ref, y * 10, 10)
    gather_plane(links, me, blocks)

    ones = jnp.ones((8, 256), F32)

    def products(g):
        value = blocks[g].reshape(SLICE, 256)
        wide = value.astype(F32)
        squares[g] = ones * jnp.sum(wide * wide, axis=0, keepdims=True)
        return contract(w_gate[...], value), contract(w_in[...], value)

    up, down, far = me.yo(1), me.yo(-1), me.yo(2)
    to_up, to_down, to_far = me.at(y=up), me.at(y=down), me.at(y=far)
    gate, value = products(far)
    pre_send[far, 0] = gate.astype(BF16)
    relay_gate = links.start(pre_send.at[far, 0], relay_in.at[0], to_up)
    pre_send[far, 1] = value.astype(BF16)
    relay_value = links.start(pre_send.at[far, 1], relay_in.at[1], to_down)
    square_copies = [links.start(squares.at[far], squares_in.at[0], to_far)]
    gate, value = products(up)
    pre_send[up, 0] = gate.astype(BF16)
    pre_send[up, 1] = value.astype(BF16)
    straight_up = links.start(pre_send.at[up, 1], pre_in.at[0, 1], to_up)
    square_copies.append(links.start(squares.at[up], squares_in.at[1], to_up))
    gate, value = products(down)
    pre_send[down, 0] = gate.astype(BF16)
    straight_down = links.start(pre_send.at[down, 0], pre_in.at[1, 0], to_down)
    pre_send[down, 1] = value.astype(BF16)
    square_copies.append(links.start(squares.at[down], squares_in.at[2], to_down))
    relay_gate.wait_recv()
    add_to(pre_send.at[up, 0], relay_in.at[0])
    joint_up = links.start(pre_send.at[up, 0], pre_in.at[0, 0], to_up)
    relay_value.wait_recv()
    add_to(pre_send.at[down, 1], relay_in.at[1])
    joint_down = links.start(pre_send.at[down, 1], pre_in.at[1, 1], to_down)
    gate, value = products(y)
    pre_own[0] = gate
    pre_own[1] = value
    for copy in square_copies:
        copy.wait_recv()
    total = squares[y] + squares_in[0] + squares_in[1] + squares_in[2]
    inverse = lax.rsqrt(total * (1.0 / WIDTH) + EPS)[0:1, :]
    straight_up.wait_recv()
    straight_down.wait_recv()
    joint_up.wait_recv()
    joint_down.wait_recv()
    gate = (pre_own[0] + pre_in[0, 0].astype(F32) + pre_in[1, 0].astype(F32)) * inverse
    value = (pre_own[1] + pre_in[0, 1].astype(F32) + pre_in[1, 1].astype(F32)) * inverse
    hidden[y] = (gelu(gate) * value).astype(BF16)

    half = UNITS // 2
    out_up = links.start(hidden.at[y], hidden.at[y], to_up)
    out_down = links.start(hidden.at[y], hidden.at[y], to_down)
    loads[2].wait()
    partner = me.at(c=1 - c)
    core_copies = []

    def outward(g):
        sums[g] = contract(w_out[...], hidden[g]).astype(BF16).reshape(NZ, 2, PART, 256)
        core_copies.append((g, links.start(sums.at[g, :, 1 - c], theirs.at[g], partner)))

    outward(y)
    out_up.wait_recv()
    far_up = links.start(hidden.at[down, pl.ds(0, half)], hidden.at[down, pl.ds(0, half)], to_up)
    out_down.wait_recv()
    far_down = links.start(hidden.at[up, pl.ds(half, half)], hidden.at[up, pl.ds(half, half)], to_down)
    outward(down)
    outward(up)
    far_up.wait_recv()
    far_down.wait_recv()
    outward(far)

    scatter_plane(
        links, me,
        (sums, theirs, first, both, up_z, down_z, up_tail, down_tail, tail_first, tail_both, result),
        core_copies,
    )

    @pl.when(jnp.logical_not(diagonal))
    def _():
        turns[1].wait_recv()

    encoded = (blocks[x, z, c].astype(F32) + result[...]).astype(BF16)
    baseline = base[...].astype(F32)
    difference = encoded.astype(F32) - baseline
    example = lax.broadcasted_iota(jnp.int32, (PART, 256), 1) // SEQ
    size = jnp.abs(difference)
    scale = jnp.zeros((PART, 256), F32)
    for e in range(4):
        top = jnp.max(jnp.where(example == e, size, 0.0), axis=1, keepdims=True) + EPS
        scale = jnp.where(example == e, top, scale)
    codes = (difference / scale).astype(BF16)
    code_pair[0] = (baseline + codes.astype(F32) * scale).astype(BF16)
    code_pair[1] = codes

    fans = [
        pltpu.make_async_remote_copy(
            src_ref=code_pair.at[0], dst_ref=memory_all.at[x], send_sem=fan_send.at[l], recv_sem=fan_recv.at[x],
            device_id=me.at(y=l, x=y), device_id_type=MESH)
        for l in range(4)
    ]
    code_turn = pltpu.make_async_remote_copy(
        src_ref=code_pair.at[1], dst_ref=code_in, send_sem=turn_sem.at[0, 2], recv_sem=turn_sem.at[1, 2],
        device_id=other, device_id_type=MESH)
    arrivals = [
        pltpu.make_async_remote_copy(
            src_ref=code_pair.at[0], dst_ref=memory_all.at[g], send_sem=fan_send.at[g], recv_sem=fan_recv.at[g],
            device_id=other, device_id_type=MESH)
        for g in range(4)
    ]
    for l in range(4):
        @pl.when(jnp.logical_not(jnp.logical_and(diagonal, y == l)))
        def _():
            fans[l].start()

    @pl.when(jnp.logical_not(diagonal))
    def _():
        code_turn.start()

    @pl.when(diagonal)
    def _():
        memory_all[x] = code_pair[0]
        code_in[...] = code_pair[1]

    for copy in lang_copies:
        copy.wait_recv()
    lang_all[y] = lang_send[...]
    languages_ref[...] = lang_all[...]

    for g in range(4):
        @pl.when(jnp.logical_not(jnp.logical_and(diagonal, x == g)))
        def _():
            arrivals[g].wait_recv()

    @pl.when(jnp.logical_not(diagonal))
    def _():
        code_turn.wait_recv()

    all_ref[...] = memory_all[...]
    memory_ref[...] = memory_all[y].T.reshape(4, SEQ, PART)
    quantized_ref[...] = code_in[...].T.reshape(4, SEQ, PART)

    for l in range(4):
        @pl.when(jnp.logical_not(jnp.logical_and(diagonal, y == l)))
        def _():
            fans[l].wait_send()

    @pl.when(jnp.logical_not(diagonal))
    def _():
        code_turn.wait_send()
        for turn in turns:
            turn.wait_send()

    links.finish()


def decoder_kernel(
    rows, memory_ref, language_ref, gain_ref, gate_hbm, in_hbm, out_hbm,
    decoded_ref,
    blocks, own, w_gate, w_in, w_out, hidden, acc, finished,
    sums, theirs, first, both, up_z, down_z, up_tail, down_tail, tail_first, tail_both, result,
    send_sem, recv_sem, load_sem,
):
    me = Place()
    x, y, z, c = me.x, me.y, me.z, me.c
    links = Links(send_sem, recv_sem)
    loads = [
        pltpu.make_async_copy(src, dst, load_sem.at[i])
        for i, (src, dst) in enumerate(((gate_hbm, w_gate), (in_hbm, w_in), (out_hbm, w_out)))
    ]
    for load in loads:
        load.start()

    lane = lax.broadcasted_iota(jnp.int32, (SEQ, rows), 1)
    line = lax.broadcasted_iota(jnp.int32, (SEQ, rows), 0)
    count = jnp.int32(0)
    chosen = jnp.zeros((PART, rows), F32)
    for g in range(4):
        picks = []
        for e in range(4):
            mine = language_ref[g * 4 + e] == y
            start = jnp.where(mine, count * SEQ, -SEQ)
            count = count + mine.astype(jnp.int32)
            picks.append((lane == line + start).astype(F32).astype(BF16))
        chosen = chosen + jnp.dot(memory_ref[g], jnp.concatenate(picks, axis=0), preferred_element_type=F32)
    own[...] = chosen.astype(BF16)
    blocks[x, z, c] = own[...]

    greet(me, me.plane() + me.column(), 8)
    gather = functools.partial(gather_plane, links, me, blocks)
    loads[0].wait()
    loads[1].wait()
    scale_rows((w_gate, w_in), gain_ref, 0, 40)
    gather()

    total = jnp.zeros((1, rows), F32)
    for g in range(4):
        part = pl.ds(g * SLICE, SLICE)
        value = blocks[g].reshape(SLICE, rows)
        wide = value.astype(F32)
        total = total + jnp.sum(wide * wide, axis=0, keepdims=True)
        for i, w in enumerate((w_gate, w_in)):
            term = contract(w[part, :], value)
            acc[i] = term if g == 0 else acc[i] + term
    inverse = lax.rsqrt(total * (1.0 / WIDTH) + EPS)
    hidden[...] = (gelu(acc[0] * inverse) * (acc[1] * inverse)).astype(BF16)

    loads[2].wait()
    partner = me.at(c=1 - c)
    core_copies = []
    for g in range(4):
        product = contract(w_out[:, pl.ds(g * SLICE, SLICE)], hidden[...])
        sums[g] = product.astype(BF16).reshape(NZ, 2, PART, rows)
        core_copies.append((g, links.start(sums.at[g, :, 1 - c], theirs.at[g], partner)))
    scatter_plane(
        links, me,
        (sums, theirs, first, both, up_z, down_z, up_tail, down_tail, tail_first, tail_both, result),
        core_copies,
    )
    finished[y] = (own[...].astype(F32) + result[...]).astype(BF16)
    returns = [links.start(finished.at[y], finished.at[y], me.at(y=me.yo(k))) for k in (1, 2, 3)]

    place = lax.broadcasted_iota(jnp.int32, (rows, 256), 0)
    column = lax.broadcasted_iota(jnp.int32, (rows, 256), 1)
    example, token = column // SEQ, column % SEQ
    sources = []
    for l in range(4):
        source = jnp.full((rows, 256), -1, jnp.int32)
        for e in range(4):
            lang = language_ref[y * 4 + e]
            slot = jnp.int32(0)
            for other in range(16):
                ahead = jnp.logical_and(language_ref[other] == lang, other < y * 4 + e)
                slot = slot + ahead.astype(jnp.int32)
            start = jnp.where(lang == l, slot * SEQ, -SEQ)
            source = jnp.where(example == e, token + start, source)
        sources.append((place == source).astype(F32).astype(BF16))
    for copy in returns:
        copy.wait_recv()
    answer = jnp.zeros((PART, 256), F32)
    for l in range(4):
        answer = answer + jnp.dot(finished[l], sources[l], preferred_element_type=F32)
    decoded_ref[...] = answer.astype(BF16).T.reshape(4, SEQ, PART)
    links.finish()


VMEM = pl.BlockSpec(memory_space=pltpu.VMEM)
SMEM = pl.BlockSpec(memory_space=pltpu.SMEM)
ANY = pl.BlockSpec(memory_space=pl.ANY)
DMA = pltpu.SemaphoreType.DMA


def encode(tokens, history, ids, language, gain, gate, up, out):
    sds = jax.ShapeDtypeStruct
    return pl.pallas_call(
        encoder_kernel,
        out_shape=(
            sds((4, PART, 256), BF16),
            sds((4, SEQ, PART), BF16),
            sds((4, SEQ, PART), BF16),
            sds((4, 8, 128), jnp.int32),
        ),
        in_specs=[VMEM, VMEM, SMEM, SMEM, VMEM, ANY, ANY, ANY],
        out_specs=(VMEM, VMEM, VMEM, VMEM),
        scratch_shapes=[
            pltpu.VMEM((2, PART, 256), BF16),
            pltpu.VMEM((PART, 256), BF16),
            pltpu.VMEM((NX, NZ, 2, PART, 256), BF16),
            pltpu.VMEM((SLICE, UNITS), BF16),
            pltpu.VMEM((SLICE, UNITS), BF16),
            pltpu.VMEM((UNITS, SLICE), BF16),
            pltpu.VMEM((4, 2, UNITS, 256), BF16),
            pltpu.VMEM((2, UNITS, 256), BF16),
            pltpu.VMEM((2, 2, UNITS, 256), BF16),
            pltpu.VMEM((2, UNITS, 256), F32),
            pltpu.VMEM((4, 8, 256), F32),
            pltpu.VMEM((3, 8, 256), F32),
            pltpu.VMEM((4, UNITS, 256), BF16),
            pltpu.VMEM((8, 128), jnp.int32),
            pltpu.VMEM((2, PART, 256), BF16),
            pltpu.VMEM((PART, 256), BF16),
            pltpu.VMEM((4, PART, 256), BF16),
            pltpu.VMEM((4, 8, 128), jnp.int32),
            *scatter_shapes(256),
            DMA((COPIES + 32,)),
            DMA((COPIES + 32,)),
            DMA((2, 3)),
            DMA((4,)),
            DMA((4,)),
            DMA((3,)),
        ],
        compiler_params=pltpu.CompilerParams(
            collective_id=0, has_side_effects=True, vmem_limit_bytes=56 << 20
        ),
    )(tokens, history, ids, language, gain, gate, up, out)


def decode(rows, memory, language, gain, gate, up, out):
    return pl.pallas_call(
        functools.partial(decoder_kernel, rows),
        out_shape=jax.ShapeDtypeStruct((4, SEQ, PART), BF16),
        in_specs=[VMEM, SMEM, VMEM, ANY, ANY, ANY],
        out_specs=VMEM,
        scratch_shapes=[
            pltpu.VMEM((NX, NZ, 2, PART, rows), BF16),
            pltpu.VMEM((PART, rows), BF16),
            pltpu.VMEM((WIDTH, UNITS), BF16),
            pltpu.VMEM((WIDTH, UNITS), BF16),
            pltpu.VMEM((UNITS, WIDTH), BF16),
            pltpu.VMEM((UNITS, rows), BF16),
            pltpu.VMEM((2, UNITS, rows), F32),
            pltpu.VMEM((4, PART, rows), BF16),
            *scatter_shapes(rows),
            DMA((COPIES,)),
            DMA((COPIES,)),
            DMA((3,)),
        ],
        compiler_params=pltpu.CompilerParams(
            collective_id=1, has_side_effects=True, vmem_limit_bytes=56 << 20
        ),
    )(memory, language, gain, gate, up, out)


def shards(
    tokens, language, example_ids, history, enc_gain, dec_gain, enc_gate, enc_in, enc_out, dec_gate, dec_in, dec_out
):
    memory_all, new_memory, quantized, languages = encode(
        tokens, history, example_ids, language, enc_gain.reshape(40, 128), enc_gate, enc_in, enc_out
    )
    names = languages[:, 0, :4].reshape(16)
    decoded = decode(
        8 * SEQ, memory_all, names, dec_gain.reshape(40, 128), dec_gate[0], dec_in[0], dec_out[0]
    )
    return decoded, new_memory, quantized


def solution(mesh):
    in_specs = (
        P("section", None, "tp"),
        P("section", None),
        P("section"),
        P(None, None, "tp"),
        P(),
        P("section", None),
        P("section", "tp"),
        P("section", "tp"),
        P("tp", "section"),
        P("section", None, "tp"),
        P("section", None, "tp"),
        P("section", "tp", None),
    )
    out_specs = (P("section", None, "tp"), P("section", None, "tp"), P("section", None, "tp"))
    return jax.shard_map(shards, mesh=mesh, in_specs=in_specs, out_specs=out_specs, check_vma=False)
```

time: 671 us -> 208 us (0.31)
  waiting for transfers between devices: 583 us -> 0 us
  Pallas kernels: 0 us -> 188 us
  matrix products: 29.5 us -> 0 us
  between operations: 14.2 us -> 0.65 us
  other arithmetic: 12.2 us -> 0 us
  blocking collectives: 9.99 us -> 0 us
    reduce_scatter x2 -> x0, waiting for transfers between devices: 294 us -> none  [the longest x1 154 us: shards(): lax.psum_scatter(partial_out, 'tp', scatter_dimension=1, tiled=True)]
    all_gather x5 -> x0, waiting for transfers between devices: 283 us -> none  [the longest x1 79.9 us: shards(): gathered = lax.all_gather(flattened, 'tp', axis=1, tiled=True)]
    pallas_call x0 -> x2, Pallas kernels: none -> 188 us  [the longest x1 98.3 us: encode(): pl.pallas_call(encoder_kernel, out_shape=(sds((4, PART, 256), BF16), sds(...]
    dot_general x7 -> x0, matrix products: 29.5 us -> none  [the longest x1 10.3 us: shards(): jnp.dot(hidden, lax.all_gather(enc_out, 'section', axis=1, tiled=True), p...]
    unnamed x20 -> x14, local copies, waits for them, and re-layouts: 1.42 us -> 18.1 us
    all_to_all x1 -> x0, blocking collectives: 9.99 us -> none  [shards(): lax.all_to_all(packed, 'section', split_axis=0, concat_axis=0, tiled=True)]
    reshape x7 -> x0, local copies, waits for them, and re-layouts: 8.56 us -> none  [the longest x2 3.36 us: shards(): pieces = slot_rows.reshape(row_total, width_part)]
  transfers between devices with their start and end apart: 8 -> 0, of which waited for: 8 -> 0; matrix products, arithmetic and copies ran while one was open for 2% -> 0% of each run, Pallas kernels for 0% -> 0%
where the time goes in v1:
time: 208 us
  Pallas kernels  188 us (90%)
  local copies, waits for them, and re-layouts  19.4 us (9%)
    pallas_call x1, Pallas kernels, encode(): pl.pallas_call(encoder_kernel, out_shape=(sds((4, PART, 256), BF16), sds(...  98.3 us
    pallas_call x1, Pallas kernels, decode(): pl.pallas_call(functools.partial(decoder_kernel, rows), out_shape=jax.Sha...  89.3 us
    unnamed x14, local copies, waits for them, and re-layouts  18.1 us

profile of v1, /device:TPU:2, one launch (start us, length us, event | category | flops | bytes accessed | tf_op | source)
XLA Modules:
  0.0 207.6 jit_solution(6341713064632176880)
XLA Ops:
  0.6 1.3 copy.15.language_ref
  1.9 0.0 copy-start
  1.9 2.4 %copy.16.gate_hbm = bf16[1280,320]{1,0:T(8,128)(2,1)} copy(bf16[1280,320]{0,1:T(8,128)(2,1)} %param.18) | data formatting | bytes 1638400 | tf_op args[6]
  4.3 2.2 %copy.17.in_hbm = bf16[1280,320]{1,0:T(8,128)(2,1)} copy(bf16[1280,320]{0,1:T(8,128)(2,1)} %param.19) | data formatting | bytes 1638400 | tf_op args[7]
  6.5 98.3 %shard_map.139 = (bf16[4,80,256]{2,1,0:T(8,128)(2,1)}, bf16[4,64,80]{2,1,0:T(8,128)(2,1)}, bf16[4,64,80]{2,1,0:T(8,128)(2,1)}, s32[4,8,128]{2,1,0:T(8,128)}) custom-call(bf16[4,64,80]{2,1,0:T(8,128)(2,1)} %tokens_ref.1, bf16[16,64,80]{2,1,0:T(8,128)(2,1)} %history_ref.1, s32[4]{0:T(128)} %ids_ref.1, s32[4,1]{1,0:T(4,128)} %copy.15.language_ref, ...), custom_call_target="tpu_custom_call" | custom-call | tf_op jit(solution)/shard_map/pallas_call | solution.py:649
  104.8 0.7 slice_reduce_fusion
  105.6 0.6 reshape_squeeze.3.language_ref
  106.2 0.0 copy-done
  106.2 3.6 %copy.18 = bf16[1,5120,320]{2,1,0:T(8,128)(2,1)} copy(bf16[1,5120,320]{1,2,0:T(8,128)(2,1)S(1)} %copy-done) | data formatting | bytes 6553600 | tf_op args[9]
  109.8 5.8 %copy.19 = bf16[1,5120,320]{2,1,0:T(8,128)(2,1)} copy(bf16[1,5120,320]{1,2,0:T(8,128)(2,1)} %param.22) | data formatting | bytes 6553600 | tf_op args[10]
  115.6 0.0 copy-start.2
  115.6 0.0 copy-start.1
  115.6 89.3 %shard_map.140 = bf16[4,64,80]{2,1,0:T(8,128)(2,1)} custom-call(bf16[4,80,256]{2,1,0:T(8,128)(2,1)} %get-tuple-element.7.memory_ref, s32[16]{0:T(128)} %reshape_squeeze.3.language_ref, f32[40,128]{1,0:T(8,128)} %bitcast.9, bf16[5120,320]{1,0:T(8,128)(2,1)} %bitcast.5, bf16[5120,320]{1,0:T(8,128)(2,1)} %bitcast.6, bf16[320,5120]{1,0:T(8,128)(2,1)} %bitcast.7), custom_call_target="tpu_custom_call" | custom-call | tf_op jit(solution)/shard_map/pallas_call | solution.py:693
  204.9 1.5 copy.23
  206.4 0.0 copy-done.2
  206.4 0.6 copy.24
  207.0 0.0 copy-done.1
  207.0 0.6 copy.25
Async XLA Ops:
  1.9 104.2 %copy-start = (bf16[1,5120,320]{1,2,0:T(8,128)(2,1)S(1)}, bf16[1,5120,320]{1,2,0:T(8,128)(2,1)}, u32[]{:S(2)}) copy-start(bf16[1,5120,320]{1,2,0:T(8,128)(2,1)} %param.21) | copy-start | bytes 9830404
  115.6 90.8 %copy-start.2 = (bf16[4,64,80]{2,1,0:T(8,128)(2,1)S(1)}, bf16[4,64,80]{2,1,0:T(8,128)(2,1)}, u32[]{:S(2)}) copy-start(bf16[4,64,80]{2,1,0:T(8,128)(2,1)} %get-tuple-element.15) | copy-start | bytes 122884
  115.6 91.4 %copy-start.1 = (bf16[4,64,80]{2,1,0:T(8,128)(2,1)S(1)}, bf16[4,64,80]{2,1,0:T(8,128)(2,1)}, u32[]{:S(2)}) copy-start(bf16[4,64,80]{2,1,0:T(8,128)(2,1)} %get-tuple-element.16) | copy-start | bytes 122884

commit v2 on v1

v2 whole, which is shorter than its diff:
```python
import functools

import jax
import jax.numpy as jnp
from jax import lax
from jax.experimental import pallas as pl
from jax.experimental.pallas import tpu as pltpu
from jax.sharding import PartitionSpec as P

MESH = pl.DeviceIdType.MESH
BF16 = jnp.bfloat16
F32 = jnp.float32
EPS = 1e-06
NX, NZ, NY = 4, 8, 4
SEQ = 64
PART = 80
HEAD = 64
TAIL = PART - HEAD
SLICE = 1280
UNITS = 320
WIDTH = 5120
COPIES = 128


class Links:
    def __init__(self, send_sem, recv_sem):
        self.send_sem, self.recv_sem = send_sem, recv_sem
        self.count = 0
        self.sent = []

    def start(self, src, dst, device):
        copy = pltpu.make_async_remote_copy(
            src_ref=src,
            dst_ref=dst,
            send_sem=self.send_sem.at[self.count],
            recv_sem=self.recv_sem.at[self.count],
            device_id=device,
            device_id_type=MESH,
        )
        self.count += 1
        copy.start()
        self.sent.append(copy)
        return copy

    def finish(self):
        for copy in self.sent:
            copy.wait_send()
        self.sent = []


class Place:
    def __init__(self):
        self.y = lax.axis_index("section")
        t = lax.axis_index("tp")
        self.x, self.z, self.c = t // 16, (t // 2) % 8, t % 2
        self.d = 1 - 2 * self.c

    def at(self, y=None, x=None, z=None, c=None):
        y = self.y if y is None else y
        x = self.x if x is None else x
        z = self.z if z is None else z
        c = self.c if c is None else c
        return (y, (x * 8 + z) * 2 + c)

    def xo(self, off):
        return (self.x + off + 8) % 4

    def yo(self, off):
        return (self.y + off + 8) % 4

    def zo(self, off):
        return (self.z + off + 8) % 8

    def plane(self):
        others = [self.at(z=self.zo(off)) for off in NEAR]
        others += [self.at(x=self.xo(k)) for k in (1, 2, 3)]
        return others + [self.at(c=1 - self.c)]

    def column(self):
        return [self.at(y=self.yo(k)) for k in (1, 2, 3)]


NEAR = (1, 7, 2, 6, 3, 5, 4)
FAR = (4, 3, 5, 2, 6, 1, 7)


class TailAlong:
    def __init__(self, links, me, tails, landed):
        self.links, self.me, self.tails, self.landed = links, me, tails, landed
        self.copies = {}

    def send(self, off, source, step):
        ref = self.tails(self.me.zo(source))
        self.copies[off] = self.links.start(ref, ref, self.me.at(z=self.me.zo(step)))

    def begin(self):
        for off in (2, 6, 1, 7):
            self.send(off, 0, off)
        self.landed(self.tails(self.me.z))

    def arrive(self, off):
        self.copies[off].wait_recv()
        self.landed(self.tails(self.me.zo(-off)))

    def relay(self):
        self.arrive(2)
        self.send(3, -2, 1)
        self.arrive(6)
        self.send(5, 2, -1)
        self.send(4, 2 * self.me.d, -2 * self.me.d)

    def finish(self):
        for off in (1, 7, 3, 5, 4):
            self.arrive(off)


def gather_plane(links, me, blocks, meanwhile):
    x, z, c = me.x, me.z, me.c
    partner = me.at(c=1 - c)

    def head(xx, zz):
        return blocks.at[xx, zz, c, pl.ds(0, HEAD)]

    def tail(xx):
        return blocks.at[xx, z, c, pl.ds(HEAD, TAIL)]

    def heads(zz):
        return blocks.at[:, zz, c, pl.ds(0, HEAD)]

    def tails(zz):
        return blocks.at[:, zz, c, pl.ds(HEAD, TAIL)]

    def send(ref, device):
        return links.start(ref, ref, device)

    core = []

    def to_core(ref):
        core.append(send(ref, partner))

    tail_along = TailAlong(links, me, tails, to_core)
    tail_cross = [send(tail(x), me.at(x=me.xo(k))) for k in (1, 2, 3)]
    order = (0,) + NEAR
    cross, second = {}, {}

    def send_cross(off):
        block = head(x, me.zo(-off))
        cross[off] = [send(block, me.at(x=me.xo(k))) for k in (1, 3)]

    def hop(i):
        off = order[i]
        for copy in cross[off]:
            copy.wait_recv()
        k = 1 if i % 2 == 0 else -1
        second[off] = send(head(me.xo(-k), me.zo(-off)), me.at(x=me.xo(k)))

    def land(i):
        off = order[i]
        second[off].wait_recv()
        to_core(heads(me.zo(-off)))

    along = {off: send(head(x, z), me.at(z=me.zo(off))) for off in NEAR}
    send_cross(0)
    meanwhile()
    for i in range(1, 8):
        along[order[i]].wait_recv()
        send_cross(order[i])
        if i == 2:
            for copy in tail_cross:
                copy.wait_recv()
            tail_along.begin()
        if i >= 3:
            hop(i - 3)
        if i == 6:
            tail_along.relay()
    for i in range(5, 8):
        land(i - 5)
        hop(i)
    for i in range(3, 8):
        land(i)
    tail_along.finish()
    for copy in core:
        copy.wait_recv()


def gather_turned(links, me, blocks, own, column, fan_send, fan_recv, meanwhile):
    x, y, z, c = me.x, me.y, me.z, me.c
    partner = me.at(c=1 - c)
    diagonal = x == y

    def fan(stage, src, dst):
        copies = []
        for k in range(4):
            copies.append(pltpu.make_async_remote_copy(
                src_ref=src, dst_ref=dst, send_sem=fan_send.at[stage, k], recv_sem=fan_recv.at[stage, y],
                device_id=me.at(x=me.xo(k), y=x), device_id_type=MESH))

        @pl.when(jnp.logical_not(diagonal))
        def _():
            copies[0].start()

        @pl.when(diagonal)
        def _():
            dst[...] = src[...]

        for copy in copies[1:]:
            copy.start()
        arrivals = []
        for j in range(4):
            g = me.yo(j)
            arrivals.append(pltpu.make_async_remote_copy(
                src_ref=src, dst_ref=dst, send_sem=fan_send.at[stage, j], recv_sem=fan_recv.at[stage, g],
                device_id=me.at(x=me.xo(1), y=x), device_id_type=MESH))
        return copies, arrivals

    def land(fans):
        @pl.when(jnp.logical_not(diagonal))
        def _():
            fans[1][0].wait_recv()

        for copy in fans[1][1:]:
            copy.wait_recv()

    def send(src, dst, device):
        return links.start(src, dst, device)

    def heads(zz):
        return blocks.at[:, zz, c, pl.ds(0, HEAD)]

    def tails(zz):
        return blocks.at[:, zz, c, pl.ds(HEAD, TAIL)]

    first = own.at[pl.ds(0, HEAD)]
    tail_fan = fan(8, own.at[pl.ds(HEAD, TAIL)], blocks.at[y, z, c, pl.ds(HEAD, TAIL)])
    along = {off: send(first, column.at[z], me.at(z=me.zo(off))) for off in NEAR}
    fans = {0: fan(0, first, blocks.at[y, z, c, pl.ds(0, HEAD)])}
    meanwhile()
    core = []

    def to_core(ref):
        core.append(send(ref, ref, partner))

    tail_along = TailAlong(links, me, tails, to_core)
    for i, off in enumerate(NEAR):
        along[off].wait_recv()
        zz = me.zo(-off)
        fans[off] = fan(i + 1, column.at[zz], blocks.at[y, zz, c, pl.ds(0, HEAD)])
        if i == 1:
            land(tail_fan)
            tail_along.begin()
    for i, off in enumerate((0,) + NEAR):
        land(fans[off])
        to_core(heads(me.zo(-off)))
        if i == 2:
            tail_along.relay()
    tail_along.finish()
    for copy in core:
        copy.wait_recv()

    def finish():
        for copies, _ in [tail_fan] + [fans[off] for off in (0,) + NEAR]:
            @pl.when(jnp.logical_not(diagonal))
            def _():
                copies[0].wait_send()

            for copy in copies[1:]:
                copy.wait_send()

    return finish


def add_to(dst, *terms):
    total = dst[...].astype(F32)
    for term in terms:
        total = total + term[...].astype(F32)
    dst[...] = total.astype(dst.dtype)


def scatter_shapes(rows):
    return [
        pltpu.VMEM((NX, NZ, 2, PART, rows), BF16),
        pltpu.VMEM((NX, NZ, PART, rows), BF16),
        pltpu.VMEM((3, NZ, HEAD, rows), BF16),
        pltpu.VMEM((7, HEAD, rows), BF16),
        pltpu.VMEM((7, NX, TAIL, rows), BF16),
        pltpu.VMEM((3, TAIL, rows), BF16),
        pltpu.VMEM((PART, rows), F32),
    ]


def scatter_plane(links, me, bufs, parts):
    sums, theirs, cross_in, along_in, tail_along_in, tail_cross_in, result = bufs
    x, z, c = me.x, me.z, me.c

    def head(xx, zz):
        return sums.at[xx, zz, c, pl.ds(0, HEAD)]

    def tail(xx):
        return sums.at[xx, z, c, pl.ds(HEAD, TAIL)]

    def tails(zz):
        return sums.at[:, zz, c, pl.ds(HEAD, TAIL)]

    for xx, copy in parts:
        copy.wait_recv()
        add_to(sums.at[xx, :, c], theirs.at[xx])

    order = FAR + (0,)
    hops, direct, relayed, along, tail_along, tail_cross = {}, {}, {}, {}, {}, {}

    def tail_send(off, step):
        slot = len(tail_along)
        tail_along[slot] = links.start(tails(me.zo(off)), tail_along_in.at[slot], me.at(z=me.zo(step)))

    tail_send(3, 1)
    tail_send(5, -1)
    tail_send(4, 2 * me.d)
    for i, off in enumerate(order):
        k = 1 if i % 2 == 0 else -1
        hops[i] = links.start(head(me.xo(2), me.zo(off)), cross_in.at[0, off], me.at(x=me.xo(k)))
        direct[i] = links.start(head(me.xo(-k), me.zo(off)), cross_in.at[1, off], me.at(x=me.xo(-k)))

    def relay(i):
        off = order[i]
        k = 1 if i % 2 == 0 else -1
        hops[i].wait_recv()
        add_to(head(me.xo(k), me.zo(off)), cross_in.at[0, off])
        relayed[i] = links.start(head(me.xo(k), me.zo(off)), cross_in.at[2, off], me.at(x=me.xo(k)))

    def collect(i):
        off = order[i]
        direct[i].wait_recv()
        relayed[i].wait_recv()
        add_to(head(x, me.zo(off)), cross_in.at[1, off], cross_in.at[2, off])
        if off:
            along[off] = links.start(head(x, me.zo(off)), along_in.at[off - 1], me.at(z=me.zo(off)))

    for i in range(8):
        relay(i)
        if i == 3:
            for copy in list(tail_along.values()):
                copy.wait_recv()
            add_to(tails(me.zo(2)), tail_along_in.at[0])
            add_to(tails(me.zo(-2)), tail_along_in.at[1])
            add_to(tails(me.zo(2 * me.d)), tail_along_in.at[2])
            for step in (2, -2, 1, -1):
                tail_send(step, step)
        if i >= 4:
            collect(i - 4)
    for slot in range(3, 7):
        tail_along[slot].wait_recv()
    add_to(tails(z), *[tail_along_in.at[i] for i in range(3, 7)])
    for k in (2, 1, 3):
        tail_cross[k] = links.start(tail(me.xo(k)), tail_cross_in.at[k - 1], me.at(x=me.xo(k)))
    for i in range(4, 8):
        collect(i)
    for off in FAR:
        along[off].wait_recv()
    total = head(x, z)[...].astype(F32)
    for i in range(7):
        total = total + along_in[i].astype(F32)
    result[pl.ds(0, HEAD)] = total
    for k in (2, 1, 3):
        tail_cross[k].wait_recv()
    total = tail(x)[...].astype(F32)
    for i in range(3):
        total = total + tail_cross_in[i].astype(F32)
    result[pl.ds(HEAD, TAIL)] = total


def first_weights(w_first, gate_hbm, in_hbm):
    return [(gate_hbm, w_first.at[pl.ds(0, UNITS)]), (in_hbm, w_first.at[pl.ds(UNITS, UNITS)])]


def contract(a, b):
    return lax.dot_general(a, b, (((0,), (0,)), ((), ())), preferred_element_type=F32)


def gelu(v):
    return jax.nn.gelu(v)


def scale_columns(weights, gain_ref, first_row, count):
    def step(i, carry):
        columns = pl.ds(pl.multiple_of(i * 128, 128), 128)
        line = gain_ref[pl.ds(first_row + i, 1), :]
        weights[:, columns] = (weights[:, columns].astype(F32) * line).astype(BF16)
        return carry

    lax.fori_loop(0, count, step, 0)


def greet(me, senders, receivers_count, extra=None):
    barrier = pltpu.get_barrier_semaphore()
    for device in senders:
        pl.semaphore_signal(barrier, inc=1, device_id=device, device_id_type=MESH)
    if extra is not None:
        extra(barrier)
    pl.semaphore_wait(barrier, receivers_count)


def encoder_kernel(
    tokens_ref, history_ref, ids_ref, language_ref, gain_ref, gate_hbm, in_hbm, out_hbm,
    all_ref, memory_ref, quantized_ref, languages_ref, branch_ref,
    turned, column, base, blocks, w_first, w_out, pre_send, relay_in, pre_in, pre_own,
    squares, squares_in, squares_core, hidden, lang_send, code_pair, code_in, memory_all, lang_all,
    sums, theirs, cross_in, along_in, tail_along_in, tail_cross_in, result,
    send_sem, recv_sem, turn_sem, wide_send, wide_recv, fan_send, fan_recv, load_sem,
):
    me = Place()
    x, y, z, c = me.x, me.y, me.z, me.c
    links = Links(send_sem, recv_sem)
    diagonal = x == y

    loads = [
        pltpu.make_async_copy(src, dst, load_sem.at[i])
        for i, (src, dst) in enumerate(first_weights(w_first, gate_hbm, in_hbm) + [(out_hbm, w_out)])
    ]
    for load in loads:
        load.start()

    def fan(barrier):
        for k in range(4):
            for device in (me.at(x=y, y=me.yo(k)), me.at(x=me.xo(k), y=x)):
                if k:
                    pl.semaphore_signal(barrier, inc=1, device_id=device, device_id_type=MESH)
                else:
                    @pl.when(jnp.logical_not(diagonal))
                    def _():
                        pl.semaphore_signal(barrier, inc=1, device_id=device, device_id_type=MESH)

    turned[0] = tokens_ref[...].reshape(256, PART).T
    for e in range(4):
        turned[1, :, pl.ds(e * SEQ, SEQ)] = history_ref[ids_ref[e]].T
    lane = lax.broadcasted_iota(jnp.int32, (8, 128), 1)
    lines = jnp.zeros((8, 128), jnp.int32)
    for e in range(4):
        lines = jnp.where(lane == e, language_ref[e], lines)
    lang_send[...] = lines

    greet(me, me.plane() + me.column(), jnp.where(diagonal, 20, 22), fan)

    other = me.at(y=x, x=y)
    turn = pltpu.make_async_remote_copy(
        src_ref=turned.at[1], dst_ref=base, send_sem=turn_sem.at[0, 0], recv_sem=turn_sem.at[1, 0],
        device_id=other, device_id_type=MESH)

    def meanwhile():
        @pl.when(jnp.logical_not(diagonal))
        def _():
            turn.start()

        @pl.when(diagonal)
        def _():
            base[...] = turned[1]

        loads[0].wait()
        loads[1].wait()
        scale_columns(w_first, gain_ref, y * 10, 10)

    lang_copies = [links.start(lang_send, lang_all.at[y], me.at(y=me.yo(k))) for k in (1, 2, 3)]

    finish_gather = gather_turned(
        links, me, blocks, turned.at[0], column, wide_send, wide_recv, meanwhile)

    ones = jnp.ones((8, 256), F32)

    def products(g):
        wide = blocks[g, :, c].astype(F32).reshape(SLICE // 2, 256)
        squares[g] = ones * jnp.sum(wide * wide, axis=0, keepdims=True)
        product = jnp.dot(w_first[...], blocks[g].reshape(SLICE, 256), preferred_element_type=F32)
        return product[:UNITS], product[UNITS:]

    up, down, far = me.yo(1), me.yo(-1), me.yo(2)
    to_up, to_down, to_far = me.at(y=up), me.at(y=down), me.at(y=far)
    gate, value = products(far)
    pre_send[far, 0] = gate.astype(BF16)
    relay_gate = links.start(pre_send.at[far, 0], relay_in.at[0], to_up)
    pre_send[far, 1] = value.astype(BF16)
    relay_value = links.start(pre_send.at[far, 1], relay_in.at[1], to_down)
    square_copies = [links.start(squares.at[far], squares_in.at[0], to_far)]
    gate, value = products(up)
    pre_send[up, 0] = gate.astype(BF16)
    pre_send[up, 1] = value.astype(BF16)
    straight_up = links.start(pre_send.at[up, 1], pre_in.at[0, 1], to_up)
    square_copies.append(links.start(squares.at[up], squares_in.at[1], to_up))
    gate, value = products(down)
    pre_send[down, 0] = gate.astype(BF16)
    straight_down = links.start(pre_send.at[down, 0], pre_in.at[1, 0], to_down)
    pre_send[down, 1] = value.astype(BF16)
    square_copies.append(links.start(squares.at[down], squares_in.at[2], to_down))
    relay_gate.wait_recv()
    add_to(pre_send.at[up, 0], relay_in.at[0])
    joint_up = links.start(pre_send.at[up, 0], pre_in.at[0, 0], to_up)
    relay_value.wait_recv()
    add_to(pre_send.at[down, 1], relay_in.at[1])
    joint_down = links.start(pre_send.at[down, 1], pre_in.at[1, 1], to_down)
    gate, value = products(y)
    pre_own[0] = gate
    pre_own[1] = value
    for copy in square_copies:
        copy.wait_recv()
    squares_core[0] = squares[y] + squares_in[0] + squares_in[1] + squares_in[2]
    core_square = links.start(squares_core.at[0], squares_core.at[1], me.at(c=1 - c))
    core_square.wait_recv()
    total = squares_core[0] + squares_core[1]
    inverse = lax.rsqrt(total * (1.0 / WIDTH) + EPS)[0:1, :]
    straight_up.wait_recv()
    straight_down.wait_recv()
    joint_up.wait_recv()
    joint_down.wait_recv()
    gate = (pre_own[0] + pre_in[0, 0].astype(F32) + pre_in[1, 0].astype(F32)) * inverse
    value = (pre_own[1] + pre_in[0, 1].astype(F32) + pre_in[1, 1].astype(F32)) * inverse
    hidden[y] = (gelu(gate) * value).astype(BF16)

    half = UNITS // 2
    out_up = links.start(hidden.at[y], hidden.at[y], to_up)
    out_down = links.start(hidden.at[y], hidden.at[y], to_down)
    loads[2].wait()
    partner = me.at(c=1 - c)
    core_copies = []

    def outward(g):
        sums[g] = contract(w_out[...], hidden[g]).astype(BF16).reshape(NZ, 2, PART, 256)
        core_copies.append((g, links.start(sums.at[g, :, 1 - c], theirs.at[g], partner)))

    outward(y)
    out_up.wait_recv()
    far_up = links.start(hidden.at[down, pl.ds(0, half)], hidden.at[down, pl.ds(0, half)], to_up)
    out_down.wait_recv()
    far_down = links.start(hidden.at[up, pl.ds(half, half)], hidden.at[up, pl.ds(half, half)], to_down)
    outward(down)
    outward(up)
    far_up.wait_recv()
    far_down.wait_recv()
    outward(far)

    scatter_plane(
        links, me,
        (sums, theirs, cross_in, along_in, tail_along_in, tail_cross_in, result),
        core_copies,
    )

    @pl.when(jnp.logical_not(diagonal))
    def _():
        turn.wait_recv()

    encoded = (blocks[x, z, c].astype(F32) + result[...]).astype(BF16)
    baseline = base[...].astype(F32)
    difference = encoded.astype(F32) - baseline
    example = lax.broadcasted_iota(jnp.int32, (PART, 256), 1) // SEQ
    size = jnp.abs(difference)
    scale = jnp.zeros((PART, 256), F32)
    for e in range(4):
        top = jnp.max(jnp.where(example == e, size, 0.0), axis=1, keepdims=True) + EPS
        scale = jnp.where(example == e, top, scale)
    codes = (difference / scale).astype(BF16)
    code_pair[0] = (baseline + codes.astype(F32) * scale).astype(BF16)
    code_pair[1] = codes

    fans = [
        pltpu.make_async_remote_copy(
            src_ref=code_pair.at[0], dst_ref=memory_all.at[x], send_sem=fan_send.at[l], recv_sem=fan_recv.at[x],
            device_id=me.at(y=l, x=y), device_id_type=MESH)
        for l in range(4)
    ]
    code_turn = pltpu.make_async_remote_copy(
        src_ref=code_pair.at[1], dst_ref=code_in, send_sem=turn_sem.at[0, 1], recv_sem=turn_sem.at[1, 1],
        device_id=other, device_id_type=MESH)
    arrivals = [
        pltpu.make_async_remote_copy(
            src_ref=code_pair.at[0], dst_ref=memory_all.at[g], send_sem=fan_send.at[g], recv_sem=fan_recv.at[g],
            device_id=other, device_id_type=MESH)
        for g in range(4)
    ]
    for l in range(4):
        @pl.when(jnp.logical_not(jnp.logical_and(diagonal, y == l)))
        def _():
            fans[l].start()

    @pl.when(jnp.logical_not(diagonal))
    def _():
        code_turn.start()

    @pl.when(diagonal)
    def _():
        memory_all[x] = code_pair[0]
        code_in[...] = code_pair[1]

    for copy in lang_copies:
        copy.wait_recv()
    lang_all[y] = lang_send[...]
    languages_ref[...] = lang_all[...]
    named = jnp.where(lane < 4, lang_all[...].astype(F32), -1.0)[:, 0:1]
    most = jnp.float32(0)
    for l in range(4):
        most = jnp.maximum(most, jnp.sum((named == l).astype(F32)))
    branch_ref[0] = (most > 4).astype(jnp.int32) + (most > 6).astype(jnp.int32)

    for g in range(4):
        @pl.when(jnp.logical_not(jnp.logical_and(diagonal, x == g)))
        def _():
            arrivals[g].wait_recv()

    @pl.when(jnp.logical_not(diagonal))
    def _():
        code_turn.wait_recv()

    all_ref[...] = memory_all[...]
    memory_ref[...] = memory_all[y].T.reshape(4, SEQ, PART)
    quantized_ref[...] = code_in[...].T.reshape(4, SEQ, PART)

    for l in range(4):
        @pl.when(jnp.logical_not(jnp.logical_and(diagonal, y == l)))
        def _():
            fans[l].wait_send()

    @pl.when(jnp.logical_not(diagonal))
    def _():
        code_turn.wait_send()
        turn.wait_send()

    finish_gather()

    links.finish()


def decoder_kernel(
    rows, memory_ref, language_ref, gain_ref, gate_hbm, in_hbm, out_hbm,
    decoded_ref,
    blocks, own, w_first, w_out, hidden, acc, squares, finished,
    sums, theirs, cross_in, along_in, tail_along_in, tail_cross_in, result,
    send_sem, recv_sem, load_sem,
):
    me = Place()
    x, y, z, c = me.x, me.y, me.z, me.c
    links = Links(send_sem, recv_sem)
    loads = [
        pltpu.make_async_copy(src, dst, load_sem.at[i])
        for i, (src, dst) in enumerate(first_weights(w_first, gate_hbm, in_hbm) + [(out_hbm, w_out)])
    ]
    for load in loads:
        load.start()

    lane = lax.broadcasted_iota(jnp.int32, (SEQ, rows), 1)
    line = lax.broadcasted_iota(jnp.int32, (SEQ, rows), 0)
    count = jnp.int32(0)
    chosen = jnp.zeros((PART, rows), F32)
    for g in range(4):
        picks = []
        for e in range(4):
            mine = language_ref[g, 0, e] == y
            start = jnp.where(mine, count * SEQ, -SEQ)
            count = count + mine.astype(jnp.int32)
            picks.append((lane == line + start).astype(F32).astype(BF16))
        chosen = chosen + jnp.dot(memory_ref[g], jnp.concatenate(picks, axis=0), preferred_element_type=F32)
    own[...] = chosen.astype(BF16)
    blocks[x, z, c] = own[...]

    greet(me, me.plane() + me.column(), 14)

    def meanwhile():
        loads[0].wait()
        loads[1].wait()
        scale_columns(w_first, gain_ref, 0, 40)

    gather_plane(links, me, blocks, meanwhile)

    total = jnp.zeros((1, rows), F32)
    for g in range(4):
        wide = blocks[g, :, c].astype(F32).reshape(SLICE // 2, rows)
        total = total + jnp.sum(wide * wide, axis=0, keepdims=True)
    partner = me.at(c=1 - c)
    squares[0] = jnp.broadcast_to(total, (8, rows))
    core_square = links.start(squares.at[0], squares.at[1], partner)
    for g in range(4):
        part = pl.ds(g * SLICE, SLICE)
        term = jnp.dot(w_first[:, part], blocks[g].reshape(SLICE, rows), preferred_element_type=F32)
        acc[...] = term if g == 0 else acc[...] + term
    core_square.wait_recv()
    inverse = lax.rsqrt((squares[0] + squares[1]) * (1.0 / WIDTH) + EPS)[0:1, :]
    hidden[...] = (gelu(acc[:UNITS] * inverse) * (acc[UNITS:] * inverse)).astype(BF16)

    loads[2].wait()
    core_copies = []
    for k in (2, 1, 3, 0):
        g = me.xo(k)
        columns = pl.ds(pl.multiple_of(g * SLICE, 128), SLICE)
        product = contract(w_out[:, columns], hidden[...])
        sums[g] = product.astype(BF16).reshape(NZ, 2, PART, rows)
        core_copies.append((g, links.start(sums.at[g, :, 1 - c], theirs.at[g], partner)))
    scatter_plane(
        links, me,
        (sums, theirs, cross_in, along_in, tail_along_in, tail_cross_in, result),
        core_copies,
    )
    finished[y] = (own[...].astype(F32) + result[...]).astype(BF16)
    returns = [links.start(finished.at[y], finished.at[y], me.at(y=me.yo(k))) for k in (1, 2, 3)]

    place = lax.broadcasted_iota(jnp.int32, (rows, 256), 0)
    column = lax.broadcasted_iota(jnp.int32, (rows, 256), 1)
    example, token = column // SEQ, column % SEQ
    sources = []
    for l in range(4):
        source = jnp.full((rows, 256), -1, jnp.int32)
        for e in range(4):
            lang = language_ref[y, 0, e]
            slot = jnp.int32(0)
            for other in range(16):
                ahead = jnp.logical_and(language_ref[other // 4, 0, other % 4] == lang, other < y * 4 + e)
                slot = slot + ahead.astype(jnp.int32)
            start = jnp.where(lang == l, slot * SEQ, -SEQ)
            source = jnp.where(example == e, token + start, source)
        sources.append((place == source).astype(F32).astype(BF16))
    for copy in returns:
        copy.wait_recv()
    answer = jnp.zeros((PART, 256), F32)
    for l in range(4):
        answer = answer + jnp.dot(finished[l], sources[l], preferred_element_type=F32)
    decoded_ref[...] = answer.astype(BF16).T.reshape(4, SEQ, PART)
    links.finish()


VMEM = pl.BlockSpec(memory_space=pltpu.VMEM)
SMEM = pl.BlockSpec(memory_space=pltpu.SMEM)
ANY = pl.BlockSpec(memory_space=pl.ANY)
DMA = pltpu.SemaphoreType.DMA


def encode(tokens, history, ids, language, gain, gate, up, out):
    sds = jax.ShapeDtypeStruct
    return pl.pallas_call(
        encoder_kernel,
        out_shape=(
            sds((4, PART, 256), BF16),
            sds((4, SEQ, PART), BF16),
            sds((4, SEQ, PART), BF16),
            sds((4, 8, 128), jnp.int32),
            sds((1,), jnp.int32),
        ),
        in_specs=[VMEM, VMEM, SMEM, SMEM, VMEM, ANY, ANY, ANY],
        out_specs=(VMEM, VMEM, VMEM, VMEM, SMEM),
        scratch_shapes=[
            pltpu.VMEM((2, PART, 256), BF16),
            pltpu.VMEM((NZ, HEAD, 256), BF16),
            pltpu.VMEM((PART, 256), BF16),
            pltpu.VMEM((NX, NZ, 2, PART, 256), BF16),
            pltpu.VMEM((2 * UNITS, SLICE), BF16),
            pltpu.VMEM((UNITS, SLICE), BF16),
            pltpu.VMEM((4, 2, UNITS, 256), BF16),
            pltpu.VMEM((2, UNITS, 256), BF16),
            pltpu.VMEM((2, 2, UNITS, 256), BF16),
            pltpu.VMEM((2, UNITS, 256), F32),
            pltpu.VMEM((4, 8, 256), F32),
            pltpu.VMEM((3, 8, 256), F32),
            pltpu.VMEM((2, 8, 256), F32),
            pltpu.VMEM((4, UNITS, 256), BF16),
            pltpu.VMEM((8, 128), jnp.int32),
            pltpu.VMEM((2, PART, 256), BF16),
            pltpu.VMEM((PART, 256), BF16),
            pltpu.VMEM((4, PART, 256), BF16),
            pltpu.VMEM((4, 8, 128), jnp.int32),
            *scatter_shapes(256),
            DMA((COPIES,)),
            DMA((COPIES,)),
            DMA((2, 2)),
            DMA((9, 4)),
            DMA((9, 4)),
            DMA((4,)),
            DMA((4,)),
            DMA((3,)),
        ],
        compiler_params=pltpu.CompilerParams(
            collective_id=0, has_side_effects=True, vmem_limit_bytes=56 << 20
        ),
    )(tokens, history, ids, language, gain, gate, up, out)


def decode(rows, number, memory, language, gain, gate, up, out):
    return pl.pallas_call(
        functools.partial(decoder_kernel, rows),
        out_shape=jax.ShapeDtypeStruct((4, SEQ, PART), BF16),
        in_specs=[VMEM, SMEM, VMEM, ANY, ANY, ANY],
        out_specs=VMEM,
        scratch_shapes=[
            pltpu.VMEM((NX, NZ, 2, PART, rows), BF16),
            pltpu.VMEM((PART, rows), BF16),
            pltpu.VMEM((2 * UNITS, WIDTH), BF16),
            pltpu.VMEM((UNITS, WIDTH), BF16),
            pltpu.VMEM((UNITS, rows), BF16),
            pltpu.VMEM((2 * UNITS, rows), F32),
            pltpu.VMEM((2, 8, rows), F32),
            pltpu.VMEM((4, PART, rows), BF16),
            *scatter_shapes(rows),
            DMA((COPIES,)),
            DMA((COPIES,)),
            DMA((3,)),
        ],
        compiler_params=pltpu.CompilerParams(
            collective_id=number, has_side_effects=True, vmem_limit_bytes=56 << 20
        ),
    )(memory, language, gain, gate, up, out)


def shards(
    tokens, language, example_ids, history, enc_gain, dec_gain, enc_gate, enc_in, enc_out, dec_gate, dec_in, dec_out
):
    memory_all, new_memory, quantized, languages, branch = encode(
        tokens, history, example_ids, language.reshape(4), enc_gain.reshape(40, 128), enc_gate.T, enc_in.T, enc_out
    )
    decoded = lax.switch(
        branch[0],
        [functools.partial(decode, rows * SEQ, number) for number, rows in ((1, 4), (2, 6), (3, 8))],
        memory_all, languages, dec_gain.reshape(40, 128), dec_gate[0].T, dec_in[0].T, dec_out[0],
    )
    return decoded, new_memory, quantized


def solution(mesh):
    in_specs = (
        P("section", None, "tp"),
        P("section", None),
        P("section"),
        P(None, None, "tp"),
        P(),
        P("section", None),
        P("section", "tp"),
        P("section", "tp"),
        P("tp", "section"),
        P("section", None, "tp"),
        P("section", None, "tp"),
        P("section", "tp", None),
    )
    out_specs = (P("section", None, "tp"), P("section", None, "tp"), P("section", None, "tp"))
    return jax.shard_map(shards, mesh=mesh, in_specs=in_specs, out_specs=out_specs, check_vma=False)
```

time: 208 us -> 156 us (0.75)
  Pallas kernels: 188 us -> 150 us
  local copies, waits for them, and re-layouts: 19.4 us -> 1.9 us
    pallas_call x1, Pallas kernels: 89.3 us -> 66 us  [decode(): pl.pallas_call(functools.partial(decoder_kernel, rows), out_shape=jax.Sha...]
    unnamed x14 -> x7, local copies, waits for them, and re-layouts: 18.1 us -> 1.9 us
    pallas_call x1, Pallas kernels: 98.3 us -> 83.6 us  [encode(): pl.pallas_call(encoder_kernel, out_shape=(sds((4, PART, 256), BF16), sds(...]
where the time goes in v2:
time: 156 us; the launch traced here: 154 us
  Pallas kernels  150 us (96%)
  local copies, waits for them, and re-layouts  1.9 us (1%)
    pallas_call x1, Pallas kernels, encode(): pl.pallas_call(encoder_kernel, out_shape=(sds((4, PART, 256), BF16), sds(...  83.6 us
    pallas_call x1, Pallas kernels, decode(): pl.pallas_call(functools.partial(decoder_kernel, rows), out_shape=jax.Sha...  66 us

profile of v2, /device:TPU:2, one launch (start us, length us, event | category | flops | bytes accessed | tf_op | source)
XLA Modules:
  0.0 153.8 jit_solution(17639934855122662673)
XLA Ops:
  0.6 83.6 %shard_map.139 = (bf16[4,80,256]{2,1,0:T(8,128)(2,1)S(1)}, bf16[4,64,80]{2,1,0:T(8,128)(2,1)}, bf16[4,64,80]{2,1,0:T(8,128)(2,1)}, s32[4,8,128]{2,1,0:T(8,128)S(1)}, s32[1]{0:T(128)}) custom-call(bf16[4,64,80]{2,1,0:T(8,128)(2,1)} %tokens_ref.1, bf16[16,64,80]{2,1,0:T(8,128)(2,1)} %history_ref.1, s32[4]{0:T(128)} %ids_ref.1, s32[4]{0:T(128)} %bitcast.28, ...), custom_call_target="tpu_custom_call" | custom-call | tf_op jit(solution)/shard_map/pallas_call | solution.py:732
  84.9 0.0 copy-start.1
  84.9 0.0 copy-start
  84.9 67.0 %conditional.1 = (bf16[4,64,80]{2,1,0:T(8,128)(2,1)S(1)}) conditional(s32[]{:T(128)} %bitcast.4, (bf16[4,80,256]{2,1,0:T(8,128)(2,1)S(1)}, s32[4,8,128]{2,1,0:T(8,128)S(1)}, f32[40,128]{1,0:T(8,128)}, bf16[320,5120]{1,0:T(8,128)(2,1)}, bf16[320,5120]{1,0:T(8,128)(2,1)}, /*index=5*/bf16[320,5120]{1,0:T(8,128)(2,1)}) %tuple.33, ...), branch_computations={%region_0.0_spmd, %region_1.0_spmd, %region_2.0_spmd} | conditional | bytes 8 | solution.py:811
  85.3 66.0 %branch_1_fun.1 = bf16[4,64,80]{2,1,0:T(8,128)(2,1)S(1)} custom-call(bf16[4,80,256]{2,1,0:T(8,128)(2,1)S(1)} %get-tuple-element.46.memory_ref, s32[4,8,128]{2,1,0:T(8,128)S(1)} %get-tuple-element.47.language_ref, f32[40,128]{1,0:T(8,128)} %get-tuple-element.48.gain_ref, bf16[320,5120]{1,0:T(8,128)(2,1)} %get-tuple-element.49.gate_hbm, ...), custom_call_target="tpu_custom_call" | custom-call | tf_op jit(solution)/shard_map/cond/branch_1_fun/pallas_call | solution.py:780
  151.9 0.6 copy.21
  152.5 0.0 copy-done.1
  152.5 0.6 copy.22
  153.1 0.0 copy-done
  153.1 0.6 copy.23
Async XLA Ops:
  84.9 67.6 %copy-start.1 = (bf16[4,64,80]{2,1,0:T(8,128)(2,1)S(1)}, bf16[4,64,80]{2,1,0:T(8,128)(2,1)}, u32[]{:S(2)}) copy-start(bf16[4,64,80]{2,1,0:T(8,128)(2,1)} %get-tuple-element.75) | copy-start | bytes 122884
  84.9 68.3 %copy-start = (bf16[4,64,80]{2,1,0:T(8,128)(2,1)S(1)}, bf16[4,64,80]{2,1,0:T(8,128)(2,1)}, u32[]{:S(2)}) copy-start(bf16[4,64,80]{2,1,0:T(8,128)(2,1)} %get-tuple-element.76) | copy-start | bytes 122884

commit v3 on v2

--- a/solution.py
+++ b/solution.py
@@ -20,6 +20,7 @@
 UNITS = 320
 WIDTH = 5120
 COPIES = 128
+PAIR = 2 * SEQ
 
 
 class Links:
@@ -114,7 +115,7 @@
             self.arrive(off)
 
 
-def gather_plane(links, me, blocks, meanwhile):
+def gather_plane(links, me, blocks, meanwhile, seen):
     x, z, c = me.x, me.z, me.c
     partner = me.at(c=1 - c)
 
@@ -137,6 +138,7 @@
 
     def to_core(ref):
         core.append(send(ref, partner))
+        seen(ref)
 
     tail_along = TailAlong(links, me, tails, to_core)
     tail_cross = [send(tail(x), me.at(x=me.xo(k))) for k in (1, 2, 3)]
@@ -161,8 +163,8 @@
 
     along = {off: send(head(x, z), me.at(z=me.zo(off))) for off in NEAR}
     send_cross(0)
-    meanwhile()
     for i in range(1, 8):
+        meanwhile(i - 1)
         along[order[i]].wait_recv()
         send_cross(order[i])
         if i == 2:
@@ -173,6 +175,7 @@
             hop(i - 3)
         if i == 6:
             tail_along.relay()
+    meanwhile(7)
     for i in range(5, 8):
         land(i - 5)
         hop(i)
@@ -345,14 +348,14 @@
             add_to(tails(me.zo(2 * me.d)), tail_along_in.at[2])
             for step in (2, -2, 1, -1):
                 tail_send(step, step)
-        if i >= 4:
-            collect(i - 4)
+        if i >= 2:
+            collect(i - 2)
     for slot in range(3, 7):
         tail_along[slot].wait_recv()
     add_to(tails(z), *[tail_along_in.at[i] for i in range(3, 7)])
     for k in (2, 1, 3):
         tail_cross[k] = links.start(tail(me.xo(k)), tail_cross_in.at[k - 1], me.at(x=me.xo(k)))
-    for i in range(4, 8):
+    for i in range(6, 8):
         collect(i)
     for off in FAR:
         along[off].wait_recv()
@@ -380,30 +383,30 @@
     return jax.nn.gelu(v)
 
 
-def scale_columns(weights, gain_ref, first_row, count):
+def scale_columns(weights, gain_ref, first_row, first, count):
     def step(i, carry):
-        columns = pl.ds(pl.multiple_of(i * 128, 128), 128)
-        line = gain_ref[pl.ds(first_row + i, 1), :]
+        columns = pl.ds(pl.multiple_of((first + i) * 128, 128), 128)
+        line = gain_ref[pl.ds(first_row + first + i, 1), :]
         weights[:, columns] = (weights[:, columns].astype(F32) * line).astype(BF16)
         return carry
 
     lax.fori_loop(0, count, step, 0)
 
 
-def greet(me, senders, receivers_count, extra=None):
+def greet(senders, extra=None):
     barrier = pltpu.get_barrier_semaphore()
     for device in senders:
         pl.semaphore_signal(barrier, inc=1, device_id=device, device_id_type=MESH)
     if extra is not None:
         extra(barrier)
-    pl.semaphore_wait(barrier, receivers_count)
+    return barrier
 
 
 def encoder_kernel(
     tokens_ref, history_ref, ids_ref, language_ref, gain_ref, gate_hbm, in_hbm, out_hbm,
-    all_ref, memory_ref, quantized_ref, languages_ref, branch_ref,
+    all_ref, pair_ref, languages_ref, branch_ref,
     turned, column, base, blocks, w_first, w_out, pre_send, relay_in, pre_in, pre_own,
-    squares, squares_in, squares_core, hidden, lang_send, code_pair, code_in, memory_all, lang_all,
+    squares, squares_in, squares_core, hidden, lang_send, fan_out, memory_all, lang_all,
     sums, theirs, cross_in, along_in, tail_along_in, tail_cross_in, result,
     send_sem, recv_sem, turn_sem, wide_send, wide_recv, fan_send, fan_recv, load_sem,
 ):
@@ -429,6 +432,7 @@
                     def _():
                         pl.semaphore_signal(barrier, inc=1, device_id=device, device_id_type=MESH)
 
+    barrier = greet(me.plane() + me.column(), fan)
     turned[0] = tokens_ref[...].reshape(256, PART).T
     for e in range(4):
         turned[1, :, pl.ds(e * SEQ, SEQ)] = history_ref[ids_ref[e]].T
@@ -438,7 +442,7 @@
         lines = jnp.where(lane == e, language_ref[e], lines)
     lang_send[...] = lines
 
-    greet(me, me.plane() + me.column(), jnp.where(diagonal, 20, 22), fan)
+    pl.semaphore_wait(barrier, jnp.where(diagonal, 20, 22))
 
     other = me.at(y=x, x=y)
     turn = pltpu.make_async_remote_copy(
@@ -456,7 +460,7 @@
 
         loads[0].wait()
         loads[1].wait()
-        scale_columns(w_first, gain_ref, y * 10, 10)
+        scale_columns(w_first, gain_ref, y * 10, 0, 10)
 
     lang_copies = [links.start(lang_send, lang_all.at[y], me.at(y=me.yo(k))) for k in (1, 2, 3)]
 
@@ -466,10 +470,12 @@
     ones = jnp.ones((8, 256), F32)
 
     def products(g):
+        product = jnp.dot(w_first[...], blocks[g].reshape(SLICE, 256), preferred_element_type=F32)
+        return product[:UNITS], product[UNITS:]
+
+    def measure(g):
         wide = blocks[g, :, c].astype(F32).reshape(SLICE // 2, 256)
         squares[g] = ones * jnp.sum(wide * wide, axis=0, keepdims=True)
-        product = jnp.dot(w_first[...], blocks[g].reshape(SLICE, 256), preferred_element_type=F32)
-        return product[:UNITS], product[UNITS:]
 
     up, down, far = me.yo(1), me.yo(-1), me.yo(2)
     to_up, to_down, to_far = me.at(y=up), me.at(y=down), me.at(y=far)
@@ -478,16 +484,19 @@
     relay_gate = links.start(pre_send.at[far, 0], relay_in.at[0], to_up)
     pre_send[far, 1] = value.astype(BF16)
     relay_value = links.start(pre_send.at[far, 1], relay_in.at[1], to_down)
+    measure(far)
     square_copies = [links.start(squares.at[far], squares_in.at[0], to_far)]
     gate, value = products(up)
     pre_send[up, 0] = gate.astype(BF16)
     pre_send[up, 1] = value.astype(BF16)
     straight_up = links.start(pre_send.at[up, 1], pre_in.at[0, 1], to_up)
+    measure(up)
     square_copies.append(links.start(squares.at[up], squares_in.at[1], to_up))
     gate, value = products(down)
     pre_send[down, 0] = gate.astype(BF16)
     straight_down = links.start(pre_send.at[down, 0], pre_in.at[1, 0], to_down)
     pre_send[down, 1] = value.astype(BF16)
+    measure(down)
     square_copies.append(links.start(squares.at[down], squares_in.at[2], to_down))
     relay_gate.wait_recv()
     add_to(pre_send.at[up, 0], relay_in.at[0])
@@ -496,8 +505,24 @@
     add_to(pre_send.at[down, 1], relay_in.at[1])
     joint_down = links.start(pre_send.at[down, 1], pre_in.at[1, 1], to_down)
     gate, value = products(y)
+    measure(y)
     pre_own[0] = gate
     pre_own[1] = value
+    for copy in lang_copies:
+        copy.wait_recv()
+    lang_all[y] = lang_send[...]
+    for g in range(4):
+        names = lang_all[g].astype(F32)
+        for e in range(4):
+            name = jnp.max(jnp.where(lane == e, names, 0.0)).astype(jnp.int32)
+            languages_ref[g * 4 + e] = name
+    most = jnp.int32(0)
+    for l in range(4):
+        load = jnp.int32(0)
+        for i in range(16):
+            load = load + (languages_ref[i] == l).astype(jnp.int32)
+        most = jnp.maximum(most, load)
+    branch_ref[0] = (most > 4).astype(jnp.int32) + (most > 6).astype(jnp.int32)
     for copy in square_copies:
         copy.wait_recv()
     squares_core[0] = squares[y] + squares_in[0] + squares_in[1] + squares_in[2]
@@ -514,8 +539,13 @@
     hidden[y] = (gelu(gate) * value).astype(BF16)
 
     half = UNITS // 2
-    out_up = links.start(hidden.at[y], hidden.at[y], to_up)
-    out_down = links.start(hidden.at[y], hidden.at[y], to_down)
+    low, high = pl.ds(0, half), pl.ds(half, half)
+
+    def units(g, part, device):
+        return links.start(hidden.at[g, part], hidden.at[g, part], device)
+
+    low_up, high_down = units(y, low, to_up), units(y, high, to_down)
+    high_up, low_down = units(y, high, to_up), units(y, low, to_down)
     loads[2].wait()
     partner = me.at(c=1 - c)
     core_copies = []
@@ -524,13 +554,22 @@
         sums[g] = contract(w_out[...], hidden[g]).astype(BF16).reshape(NZ, 2, PART, 256)
         core_copies.append((g, links.start(sums.at[g, :, 1 - c], theirs.at[g], partner)))
 
+    def join():
+        g, copy = core_copies.pop(0)
+        copy.wait_recv()
+        add_to(sums.at[g, :, c], theirs.at[g])
+
     outward(y)
-    out_up.wait_recv()
-    far_up = links.start(hidden.at[down, pl.ds(0, half)], hidden.at[down, pl.ds(0, half)], to_up)
-    out_down.wait_recv()
-    far_down = links.start(hidden.at[up, pl.ds(half, half)], hidden.at[up, pl.ds(half, half)], to_down)
+    low_up.wait_recv()
+    far_up = units(down, low, to_up)
+    high_down.wait_recv()
+    far_down = units(up, high, to_down)
+    high_up.wait_recv()
     outward(down)
+    low_down.wait_recv()
     outward(up)
+    for _ in range(3):
+        join()
     far_up.wait_recv()
     far_down.wait_recv()
     outward(far)
@@ -555,60 +594,44 @@
         top = jnp.max(jnp.where(example == e, size, 0.0), axis=1, keepdims=True) + EPS
         scale = jnp.where(example == e, top, scale)
     codes = (difference / scale).astype(BF16)
-    code_pair[0] = (baseline + codes.astype(F32) * scale).astype(BF16)
-    code_pair[1] = codes
-
-    fans = [
-        pltpu.make_async_remote_copy(
-            src_ref=code_pair.at[0], dst_ref=memory_all.at[x], send_sem=fan_send.at[l], recv_sem=fan_recv.at[x],
+    memory = (baseline + codes.astype(F32) * scale).astype(BF16)
+    pair_ref[0] = memory
+    pair_ref[1] = codes
+
+    slot_lane = lax.broadcasted_iota(jnp.int32, (SEQ, PAIR), 1)
+    slot_line = lax.broadcasted_iota(jnp.int32, (SEQ, PAIR), 0)
+    for l in range(4):
+        count, picks = jnp.int32(0), []
+        for e in range(4):
+            named = languages_ref[x * 4 + e] == l
+            start = jnp.where(named, count * SEQ, -SEQ)
+            count = count + named.astype(jnp.int32)
+            picks.append((slot_lane == slot_line + start).astype(F32).astype(BF16))
+        picked = jnp.dot(memory, jnp.concatenate(picks, axis=0), preferred_element_type=F32)
+        fan_out[l] = picked.astype(BF16)
+
+    def fan_copy(l, g):
+        return pltpu.make_async_remote_copy(
+            src_ref=fan_out.at[l], dst_ref=memory_all.at[g], send_sem=fan_send.at[l], recv_sem=fan_recv.at[g],
             device_id=me.at(y=l, x=y), device_id_type=MESH)
-        for l in range(4)
-    ]
-    code_turn = pltpu.make_async_remote_copy(
-        src_ref=code_pair.at[1], dst_ref=code_in, send_sem=turn_sem.at[0, 1], recv_sem=turn_sem.at[1, 1],
-        device_id=other, device_id_type=MESH)
-    arrivals = [
-        pltpu.make_async_remote_copy(
-            src_ref=code_pair.at[0], dst_ref=memory_all.at[g], send_sem=fan_send.at[g], recv_sem=fan_recv.at[g],
-            device_id=other, device_id_type=MESH)
-        for g in range(4)
-    ]
+
+    fans = [fan_copy(l, x) for l in range(4)]
+    arrivals = [fan_copy(g, g) for g in range(4)]
     for l in range(4):
         @pl.when(jnp.logical_not(jnp.logical_and(diagonal, y == l)))
         def _():
             fans[l].start()
 
-    @pl.when(jnp.logical_not(diagonal))
-    def _():
-        code_turn.start()
-
     @pl.when(diagonal)
     def _():
-        memory_all[x] = code_pair[0]
-        code_in[...] = code_pair[1]
-
-    for copy in lang_copies:
-        copy.wait_recv()
-    lang_all[y] = lang_send[...]
-    languages_ref[...] = lang_all[...]
-    named = jnp.where(lane < 4, lang_all[...].astype(F32), -1.0)[:, 0:1]
-    most = jnp.float32(0)
-    for l in range(4):
-        most = jnp.maximum(most, jnp.sum((named == l).astype(F32)))
-    branch_ref[0] = (most > 4).astype(jnp.int32) + (most > 6).astype(jnp.int32)
+        memory_all[x] = fan_out[y]
 
     for g in range(4):
         @pl.when(jnp.logical_not(jnp.logical_and(diagonal, x == g)))
         def _():
             arrivals[g].wait_recv()
 
-    @pl.when(jnp.logical_not(diagonal))
-    def _():
-        code_turn.wait_recv()
-
     all_ref[...] = memory_all[...]
-    memory_ref[...] = memory_all[y].T.reshape(4, SEQ, PART)
-    quantized_ref[...] = code_in[...].T.reshape(4, SEQ, PART)
 
     for l in range(4):
         @pl.when(jnp.logical_not(jnp.logical_and(diagonal, y == l)))
@@ -617,24 +640,31 @@
 
     @pl.when(jnp.logical_not(diagonal))
     def _():
-        code_turn.wait_send()
         turn.wait_send()
 
     finish_gather()
-
     links.finish()
 
 
 def decoder_kernel(
-    rows, memory_ref, language_ref, gain_ref, gate_hbm, in_hbm, out_hbm,
-    decoded_ref,
-    blocks, own, w_first, w_out, hidden, acc, squares, finished,
+    rows, memory_ref, pair_ref, language_ref, gain_ref, gate_hbm, in_hbm, out_hbm,
+    decoded_ref, new_memory_ref, quantized_ref,
+    blocks, own, w_first, w_out, hidden, acc, squares, finished, home,
     sums, theirs, cross_in, along_in, tail_along_in, tail_cross_in, result,
-    send_sem, recv_sem, load_sem,
+    send_sem, recv_sem, turn_sem, load_sem,
 ):
     me = Place()
     x, y, z, c = me.x, me.y, me.z, me.c
     links = Links(send_sem, recv_sem)
+    diagonal = x == y
+    other = me.at(y=x, x=y)
+
+    def greet_other(barrier):
+        @pl.when(jnp.logical_not(diagonal))
+        def _():
+            pl.semaphore_signal(barrier, inc=1, device_id=other, device_id_type=MESH)
+
+    barrier = greet(me.plane() + me.column(), greet_other)
     loads = [
         pltpu.make_async_copy(src, dst, load_sem.at[i])
         for i, (src, dst) in enumerate(first_weights(w_first, gate_hbm, in_hbm) + [(out_hbm, w_out)])
@@ -644,34 +674,49 @@
 
     lane = lax.broadcasted_iota(jnp.int32, (SEQ, rows), 1)
     line = lax.broadcasted_iota(jnp.int32, (SEQ, rows), 0)
-    count = jnp.int32(0)
+    number = jnp.int32(0)
     chosen = jnp.zeros((PART, rows), F32)
     for g in range(4):
+        count = jnp.int32(0)
+        for e in range(4):
+            count = count + (language_ref[g * 4 + e] == y).astype(jnp.int32)
         picks = []
-        for e in range(4):
-            mine = language_ref[g, 0, e] == y
-            start = jnp.where(mine, count * SEQ, -SEQ)
-            count = count + mine.astype(jnp.int32)
+        for j in range(2):
+            start = jnp.where(count > j, (number + j) * SEQ, -SEQ)
             picks.append((lane == line + start).astype(F32).astype(BF16))
+        number = number + count
         chosen = chosen + jnp.dot(memory_ref[g], jnp.concatenate(picks, axis=0), preferred_element_type=F32)
     own[...] = chosen.astype(BF16)
     blocks[x, z, c] = own[...]
 
-    greet(me, me.plane() + me.column(), 14)
-
-    def meanwhile():
-        loads[0].wait()
-        loads[1].wait()
-        scale_columns(w_first, gain_ref, 0, 40)
-
-    gather_plane(links, me, blocks, meanwhile)
-
-    total = jnp.zeros((1, rows), F32)
-    for g in range(4):
-        wide = blocks[g, :, c].astype(F32).reshape(SLICE // 2, rows)
-        total = total + jnp.sum(wide * wide, axis=0, keepdims=True)
+    pl.semaphore_wait(barrier, jnp.where(diagonal, 14, 15))
+
+    turn = pltpu.make_async_remote_copy(
+        src_ref=pair_ref, dst_ref=home, send_sem=turn_sem.at[0], recv_sem=turn_sem.at[1],
+        device_id=other, device_id_type=MESH)
+
+    def meanwhile(i):
+        if i == 0:
+            @pl.when(jnp.logical_not(diagonal))
+            def _():
+                turn.start()
+
+            @pl.when(diagonal)
+            def _():
+                home[...] = pair_ref[...]
+
+            loads[0].wait()
+            loads[1].wait()
+        scale_columns(w_first, gain_ref, 0, 5 * i, 5)
+
+    squares[0] = jnp.zeros((8, rows), F32)
+
+    def seen(ref):
+        wide = ref[...].astype(F32)
+        squares[0] = squares[0] + jnp.sum(wide * wide, axis=(0, 1))[None, :]
+
+    gather_plane(links, me, blocks, meanwhile, seen)
     partner = me.at(c=1 - c)
-    squares[0] = jnp.broadcast_to(total, (8, rows))
     core_square = links.start(squares.at[0], squares.at[1], partner)
     for g in range(4):
         part = pl.ds(g * SLICE, SLICE)
@@ -704,20 +749,32 @@
     for l in range(4):
         source = jnp.full((rows, 256), -1, jnp.int32)
         for e in range(4):
-            lang = language_ref[y, 0, e]
+            lang = language_ref[y * 4 + e]
             slot = jnp.int32(0)
-            for other in range(16):
-                ahead = jnp.logical_and(language_ref[other // 4, 0, other % 4] == lang, other < y * 4 + e)
+            for i in range(16):
+                ahead = jnp.logical_and(language_ref[i] == lang, i < y * 4 + e)
                 slot = slot + ahead.astype(jnp.int32)
             start = jnp.where(lang == l, slot * SEQ, -SEQ)
             source = jnp.where(example == e, token + start, source)
         sources.append((place == source).astype(F32).astype(BF16))
+
+    @pl.when(jnp.logical_not(diagonal))
+    def _():
+        turn.wait_recv()
+
+    new_memory_ref[...] = home[0].T.reshape(4, SEQ, PART)
+    quantized_ref[...] = home[1].T.reshape(4, SEQ, PART)
     for copy in returns:
         copy.wait_recv()
     answer = jnp.zeros((PART, 256), F32)
     for l in range(4):
         answer = answer + jnp.dot(finished[l], sources[l], preferred_element_type=F32)
     decoded_ref[...] = answer.astype(BF16).T.reshape(4, SEQ, PART)
+
+    @pl.when(jnp.logical_not(diagonal))
+    def _():
+        turn.wait_send()
+
     links.finish()
 
 
@@ -732,14 +789,13 @@
     return pl.pallas_call(
         encoder_kernel,
         out_shape=(
-            sds((4, PART, 256), BF16),
-            sds((4, SEQ, PART), BF16),
-            sds((4, SEQ, PART), BF16),
-            sds((4, 8, 128), jnp.int32),
+            sds((4, PART, PAIR), BF16),
+            sds((2, PART, 256), BF16),
+            sds((16,), jnp.int32),
             sds((1,), jnp.int32),
         ),
         in_specs=[VMEM, VMEM, SMEM, SMEM, VMEM, ANY, ANY, ANY],
-        out_specs=(VMEM, VMEM, VMEM, VMEM, SMEM),
+        out_specs=(VMEM, VMEM, SMEM, SMEM),
         scratch_shapes=[
             pltpu.VMEM((2, PART, 256), BF16),
             pltpu.VMEM((NZ, HEAD, 256), BF16),
@@ -756,14 +812,13 @@
             pltpu.VMEM((2, 8, 256), F32),
             pltpu.VMEM((4, UNITS, 256), BF16),
             pltpu.VMEM((8, 128), jnp.int32),
-            pltpu.VMEM((2, PART, 256), BF16),
-            pltpu.VMEM((PART, 256), BF16),
-            pltpu.VMEM((4, PART, 256), BF16),
+            pltpu.VMEM((4, PART, PAIR), BF16),
+            pltpu.VMEM((4, PART, PAIR), BF16),
             pltpu.VMEM((4, 8, 128), jnp.int32),
             *scatter_shapes(256),
             DMA((COPIES,)),
             DMA((COPIES,)),
-            DMA((2, 2)),
+            DMA((2, 1)),
             DMA((9, 4)),
             DMA((9, 4)),
             DMA((4,)),
@@ -776,12 +831,12 @@
     )(tokens, history, ids, language, gain, gate, up, out)
 
 
-def decode(rows, number, memory, language, gain, gate, up, out):
+def decode(rows, number, memory, pair, language, gain, gate, up, out):
     return pl.pallas_call(
         functools.partial(decoder_kernel, rows),
-        out_shape=jax.ShapeDtypeStruct((4, SEQ, PART), BF16),
-        in_specs=[VMEM, SMEM, VMEM, ANY, ANY, ANY],
-        out_specs=VMEM,
+        out_shape=(jax.ShapeDtypeStruct((4, SEQ, PART), BF16),) * 3,
+        in_specs=[VMEM, VMEM, SMEM, VMEM, ANY, ANY, ANY],
+        out_specs=(VMEM, VMEM, VMEM),
         scratch_shapes=[
             pltpu.VMEM((NX, NZ, 2, PART, rows), BF16),
             pltpu.VMEM((PART, rows), BF16),
@@ -791,29 +846,30 @@
             pltpu.VMEM((2 * UNITS, rows), F32),
             pltpu.VMEM((2, 8, rows), F32),
             pltpu.VMEM((4, PART, rows), BF16),
+            pltpu.VMEM((2, PART, 256), BF16),
             *scatter_shapes(rows),
             DMA((COPIES,)),
             DMA((COPIES,)),
+            DMA((2,)),
             DMA((3,)),
         ],
         compiler_params=pltpu.CompilerParams(
             collective_id=number, has_side_effects=True, vmem_limit_bytes=56 << 20
         ),
-    )(memory, language, gain, gate, up, out)
+    )(memory, pair, language, gain, gate, up, out)
 
 
 def shards(
     tokens, language, example_ids, history, enc_gain, dec_gain, enc_gate, enc_in, enc_out, dec_gate, dec_in, dec_out
 ):
-    memory_all, new_memory, quantized, languages, branch = encode(
+    memory_all, pair, languages, branch = encode(
         tokens, history, example_ids, language.reshape(4), enc_gain.reshape(40, 128), enc_gate.T, enc_in.T, enc_out
     )
-    decoded = lax.switch(
+    return lax.switch(
         branch[0],
         [functools.partial(decode, rows * SEQ, number) for number, rows in ((1, 4), (2, 6), (3, 8))],
-        memory_all, languages, dec_gain.reshape(40, 128), dec_gate[0].T, dec_in[0].T, dec_out[0],
+        memory_all, pair, languages, dec_gain.reshape(40, 128), dec_gate[0].T, dec_in[0].T, dec_out[0],
     )
-    return decoded, new_memory, quantized
 
 
 def solution(mesh):

time: 156 us -> 152 us (0.974); the launches traced: 154 us -> 152 us
  Pallas kernels: 150 us -> 148 us
where the time goes in v3:
time: 152 us
  Pallas kernels  148 us (97%)
  local copies, waits for them, and re-layouts  1.89 us (1%)
    pallas_call x1, Pallas kernels, encode(): pl.pallas_call(encoder_kernel, out_shape=(sds((4, PART, PAIR), BF16), sds...  79.4 us
    pallas_call x1, Pallas kernels, decode(): pl.pallas_call(functools.partial(decoder_kernel, rows), out_shape=(jax.Sh...  68.9 us

profile of v3, /device:TPU:2, one launch (start us, length us, event | category | flops | bytes accessed | tf_op | source)
XLA Modules:
  0.0 152.0 jit_solution(15291789123407127634)
XLA Ops:
  0.6 79.4 %shard_map.154 = (bf16[4,80,128]{2,1,0:T(8,128)(2,1)S(1)}, bf16[2,80,256]{2,1,0:T(8,128)(2,1)S(1)}, s32[16]{0:T(128)S(1)}, s32[1]{0:T(128)}) custom-call(bf16[4,64,80]{2,1,0:T(8,128)(2,1)} %tokens_ref.1, bf16[16,64,80]{2,1,0:T(8,128)(2,1)} %history_ref.1, s32[4]{0:T(128)} %ids_ref.1, s32[4]{0:T(128)} %bitcast.32, f32[40,128]{1,0:T(8,128)} %bitcast.31, ...), custom_call_target="tpu_custom_call" | custom-call | tf_op jit(solution)/shard_map/pallas_call | solution.py:789
  80.6 69.5 %conditional.1 = ((bf16[4,64,80]{2,1,0:T(8,128)(2,1)S(1)}, bf16[4,64,80]{2,1,0:T(8,128)(2,1)S(1)}, bf16[4,64,80]{2,1,0:T(8,128)(2,1)S(1)})) conditional(s32[]{:T(128)} %bitcast.10, (bf16[4,80,128]{2,1,0:T(8,128)(2,1)S(1)}, bf16[2,80,256]{2,1,0:T(8,128)(2,1)S(1)}, s32[16]{0:T(128)S(1)}, f32[1,5120]{1,0:T(1,128)}, ...), branch_computations={%region_0.0_spmd, %region_1.0_spmd, %region_2.0_spmd} | conditional | bytes 8 | solution.py:868
  80.9 68.9 %branch_1_fun.1 = (bf16[4,64,80]{2,1,0:T(8,128)(2,1)S(1)}, bf16[4,64,80]{2,1,0:T(8,128)(2,1)S(1)}, bf16[4,64,80]{2,1,0:T(8,128)(2,1)S(1)}) custom-call(bf16[4,80,128]{2,1,0:T(8,128)(2,1)S(1)} %get-tuple-element.49.memory_ref, bf16[2,80,256]{2,1,0:T(8,128)(2,1)S(1)} %get-tuple-element.50.pair_ref, s32[16]{0:T(128)S(1)} %get-tuple-element.51.language_ref, ...), custom_call_target="tpu_custom_call" | custom-call | tf_op jit(solution)/shard_map/cond/branch_1_fun/pallas_call | solution.py:835
  150.1 0.6 copy.42
  150.7 0.6 copy.43
  151.4 0.6 copy.44

commit v4 on v3

--- a/solution.py
+++ b/solution.py
@@ -16,6 +16,8 @@
 PART = 80
 HEAD = 64
 TAIL = PART - HEAD
+TURN_HEAD = 48
+TURN_TAIL = PART - TURN_HEAD
 SLICE = 1280
 UNITS = 320
 WIDTH = 5120
@@ -228,15 +230,15 @@
         return links.start(src, dst, device)
 
     def heads(zz):
-        return blocks.at[:, zz, c, pl.ds(0, HEAD)]
+        return blocks.at[:, zz, c, pl.ds(0, TURN_HEAD)]
 
     def tails(zz):
-        return blocks.at[:, zz, c, pl.ds(HEAD, TAIL)]
-
-    first = own.at[pl.ds(0, HEAD)]
-    tail_fan = fan(8, own.at[pl.ds(HEAD, TAIL)], blocks.at[y, z, c, pl.ds(HEAD, TAIL)])
+        return blocks.at[:, zz, c, pl.ds(TURN_HEAD, TURN_TAIL)]
+
+    first = own.at[pl.ds(0, TURN_HEAD)]
+    tail_fan = fan(8, own.at[pl.ds(TURN_HEAD, TURN_TAIL)], blocks.at[y, z, c, pl.ds(TURN_HEAD, TURN_TAIL)])
     along = {off: send(first, column.at[z], me.at(z=me.zo(off))) for off in NEAR}
-    fans = {0: fan(0, first, blocks.at[y, z, c, pl.ds(0, HEAD)])}
+    fans = {0: fan(0, first, blocks.at[y, z, c, pl.ds(0, TURN_HEAD)])}
     meanwhile()
     core = []
 
@@ -247,7 +249,7 @@
     for i, off in enumerate(NEAR):
         along[off].wait_recv()
         zz = me.zo(-off)
-        fans[off] = fan(i + 1, column.at[zz], blocks.at[y, zz, c, pl.ds(0, HEAD)])
+        fans[off] = fan(i + 1, column.at[zz], blocks.at[y, zz, c, pl.ds(0, TURN_HEAD)])
         if i == 1:
             land(tail_fan)
             tail_along.begin()
@@ -798,7 +800,7 @@
         out_specs=(VMEM, VMEM, SMEM, SMEM),
         scratch_shapes=[
             pltpu.VMEM((2, PART, 256), BF16),
-            pltpu.VMEM((NZ, HEAD, 256), BF16),
+            pltpu.VMEM((NZ, TURN_HEAD, 256), BF16),
             pltpu.VMEM((PART, 256), BF16),
             pltpu.VMEM((NX, NZ, 2, PART, 256), BF16),
             pltpu.VMEM((2 * UNITS, SLICE), BF16),

time: 152 us -> 150 us (0.987)
  no operation moved by 1% of the time
where the time goes in v4:
time: 150 us
  Pallas kernels  147 us (98%)
  local copies, waits for them, and re-layouts  1.89 us (1%)
    pallas_call x1, Pallas kernels, encode(): pl.pallas_call(encoder_kernel, out_shape=(sds((4, PART, PAIR), BF16), sds...  78.8 us
    pallas_call x1, Pallas kernels, decode(): pl.pallas_call(functools.partial(decoder_kernel, rows), out_shape=(jax.Sh...  67.9 us

profile of v4, /device:TPU:2, one launch (start us, length us, event | category | flops | bytes accessed | tf_op | source)
XLA Modules:
  0.0 150.3 jit_solution(6089881153137762268)
XLA Ops:
  0.6 78.8 %shard_map.154 = (bf16[4,80,128]{2,1,0:T(8,128)(2,1)S(1)}, bf16[2,80,256]{2,1,0:T(8,128)(2,1)S(1)}, s32[16]{0:T(128)S(1)}, s32[1]{0:T(128)}) custom-call(bf16[4,64,80]{2,1,0:T(8,128)(2,1)} %tokens_ref.1, bf16[16,64,80]{2,1,0:T(8,128)(2,1)} %history_ref.1, s32[4]{0:T(128)} %ids_ref.1, s32[4]{0:T(128)} %bitcast.32, f32[40,128]{1,0:T(8,128)} %bitcast.31, ...), custom_call_target="tpu_custom_call" | custom-call | tf_op jit(solution)/shard_map/pallas_call | solution.py:791
  80.0 68.4 %conditional.1 = ((bf16[4,64,80]{2,1,0:T(8,128)(2,1)S(1)}, bf16[4,64,80]{2,1,0:T(8,128)(2,1)S(1)}, bf16[4,64,80]{2,1,0:T(8,128)(2,1)S(1)})) conditional(s32[]{:T(128)} %bitcast.10, (bf16[4,80,128]{2,1,0:T(8,128)(2,1)S(1)}, bf16[2,80,256]{2,1,0:T(8,128)(2,1)S(1)}, s32[16]{0:T(128)S(1)}, f32[1,5120]{1,0:T(1,128)}, ...), branch_computations={%region_0.0_spmd, %region_1.0_spmd, %region_2.0_spmd} | conditional | bytes 8 | solution.py:870
  80.2 67.9 %branch_1_fun.1 = (bf16[4,64,80]{2,1,0:T(8,128)(2,1)S(1)}, bf16[4,64,80]{2,1,0:T(8,128)(2,1)S(1)}, bf16[4,64,80]{2,1,0:T(8,128)(2,1)S(1)}) custom-call(bf16[4,80,128]{2,1,0:T(8,128)(2,1)S(1)} %get-tuple-element.49.memory_ref, bf16[2,80,256]{2,1,0:T(8,128)(2,1)S(1)} %get-tuple-element.50.pair_ref, s32[16]{0:T(128)S(1)} %get-tuple-element.51.language_ref, ...), custom_call_target="tpu_custom_call" | custom-call | tf_op jit(solution)/shard_map/cond/branch_1_fun/pallas_call | solution.py:837
  148.4 0.6 copy.42
  149.1 0.6 copy.43
  149.7 0.6 copy.44
